TPU v7x, 32 devices: a whole 2x2x4 slice. The times are simulated.
32 devices in a mesh: dp: 2 (over x), expert: 16 (over z, y, core).
Axes of the slice: x: 2, y: 2, z: 4, core: 2. Of those that a mesh axis runs over, the one named last changes fastest.
Arguments:
- tokens: bfloat16 [4096, 2048], P(('dp', 'expert')), may hold values from -6 to 6
- expert_ids: int32 [4096], P(('dp', 'expert')), may hold values from 0 to 15
- gate: float32 [4096], P(('dp', 'expert')), may hold values from 0.2 to 1
- cotangent: bfloat16 [4096, 2048], P(('dp', 'expert')), may hold values from -6 to 6
- w_up: bfloat16 [16, 2048, 768], P('expert'), may hold values from -0.125 to 0.125
- w_down: bfloat16 [16, 768, 2048], P('expert'), may hold values from -0.21875 to 0.21875
Outputs:
- layer_out: bfloat16 [4096, 2048], P(('dp', 'expert'))
- token_grad: bfloat16 [4096, 2048], P(('dp', 'expert'))
- up_grad: float32 [16, 2048, 768], P('expert', 'dp')
- down_grad: float32 [16, 768, 2048], P('expert', None, 'dp')
All inputs are finite; a program needn't handle non-finite values.
Results may differ from a plain program's by a relative error of at most 0.013.
Values may be sent and summed in bfloat16 or wider, within the bound.
A program may use at most 64 MiB of HBM per device.

v0:
```python
import jax
import jax.numpy as jnp
from jax import lax
from jax.sharding import PartitionSpec as P


def shards(tokens, expert_ids, gate, cotangent, w_up, w_down):
    tok_rows = tokens.shape[0]
    model_width = tokens.shape[1]
    experts = lax.axis_size("expert")
    slot_count = tok_rows // experts
    onehot = (expert_ids[:, None] == jnp.arange(experts, dtype=jnp.int32)[None, :]).astype(
        jnp.int32
    )
    row_rank = jnp.sum((jnp.cumsum(onehot, axis=0) - onehot) * onehot, axis=1)
    target = jnp.where(row_rank < slot_count, expert_ids * slot_count + row_rank, -1)
    select = (target[None, :] == jnp.arange(experts * slot_count, dtype=jnp.int32)[:, None]).astype(
        jnp.bfloat16
    )
    send_x = jnp.dot(select, tokens, preferred_element_type=jnp.float32).astype(jnp.bfloat16)
    scaled = (gate[:, None] * cotangent.astype(jnp.float32)).astype(jnp.bfloat16)
    send_c = jnp.dot(select, scaled, preferred_element_type=jnp.float32).astype(jnp.bfloat16)
    send_x = send_x.reshape(experts, slot_count, model_width)
    send_c = send_c.reshape(experts, slot_count, model_width)
    w_in = w_up[0]
    w_out = w_down[0]
    arrived_x = lax.all_to_all(send_x, "expert", split_axis=0, concat_axis=0, tiled=True)
    rows_x = arrived_x.reshape(-1, model_width)
    pre_act = jnp.dot(rows_x, w_in, preferred_element_type=jnp.float32)
    hidden = jax.nn.silu(pre_act).astype(jnp.bfloat16)
    expert_out = jnp.dot(hidden, w_out, preferred_element_type=jnp.float32).astype(jnp.bfloat16)
    rows_x, pre_act, hidden, expert_out = (
        rows_x,
        pre_act,
        hidden,
        expert_out.reshape(experts, slot_count, model_width),
    )
    back_out = lax.all_to_all(expert_out, "expert", split_axis=0, concat_axis=0, tiled=True)
    arrived_c = lax.all_to_all(send_c, "expert", split_axis=0, concat_axis=0, tiled=True)
    rows_c = arrived_c.reshape(-1, model_width)
    back = lax.dot_general(
        rows_c, w_out, (((1,), (1,)), ((), ())), preferred_element_type=jnp.float32
    )
    sigma = jax.nn.sigmoid(pre_act)
    grad_pre = (back * sigma * (1.0 + pre_act * (1.0 - sigma))).astype(jnp.bfloat16)
    slot_grad = lax.dot_general(
        grad_pre, w_in, (((1,), (1,)), ((), ())), preferred_element_type=jnp.float32
    )
    rows_c, grad_pre, slot_grad = (
        rows_c,
        grad_pre,
        slot_grad.astype(jnp.bfloat16).reshape(experts, slot_count, model_width),
    )
    back_grad = lax.all_to_all(slot_grad, "expert", split_axis=0, concat_axis=0, tiled=True)
    numbers = (((0,), (0,)), ((), ()))
    out_rows = lax.dot_general(
        select, back_out.reshape(-1, model_width), numbers, preferred_element_type=jnp.float32
    )
    grad_rows = lax.dot_general(
        select, back_grad.reshape(-1, model_width), numbers, preferred_element_type=jnp.float32
    )
    layer_out = (gate[:, None] * out_rows).astype(jnp.bfloat16)
    token_grad = grad_rows.astype(jnp.bfloat16)
    groups = lax.axis_size("dp")
    shard_cols = model_width // groups
    hidden_units = hidden.shape[1]
    rows_here = rows_x.shape[0]
    cols_x, cols_c = (
        lax.all_to_all(rows_x, "dp", split_axis=1, concat_axis=0, tiled=True),
        lax.all_to_all(rows_c, "dp", split_axis=1, concat_axis=0, tiled=True),
    )
    hidden_piece = lax.all_gather(hidden, "dp", axis=0, tiled=True)
    grad_piece = lax.all_gather(grad_pre, "dp", axis=0, tiled=True)
    group_count = hidden_piece.shape[0] // rows_here
    part_x = cols_x
    part_c = cols_c
    part_x = part_x.reshape(group_count, rows_here, shard_cols)
    part_c = part_c.reshape(group_count, rows_here, shard_cols)
    hidden_piece = hidden_piece.reshape(group_count, rows_here, hidden_units)
    grad_piece = grad_piece.reshape(group_count, rows_here, hidden_units)
    up_terms = jnp.einsum("krw,krf->kwf", part_x, grad_piece, preferred_element_type=jnp.float32)
    down_terms = jnp.einsum(
        "krf,krw->kfw", hidden_piece, part_c, preferred_element_type=jnp.float32
    )
    up_sum = jnp.sum(up_terms.astype(jnp.bfloat16).astype(jnp.float32), axis=0)
    down_sum = jnp.sum(down_terms.astype(jnp.bfloat16).astype(jnp.float32), axis=0)
    sum_up = up_sum
    sum_down = down_sum
    sum_up = sum_up[None]
    sum_down = sum_down[None]
    inverse = 1.0 / lax.axis_size("dp")
    return (layer_out, token_grad, sum_up * inverse, sum_down * inverse)


def solution(mesh):
    in_specs = (
        P(("dp", "expert"), None),
        P(("dp", "expert")),
        P(("dp", "expert")),
        P(("dp", "expert"), None),
        P("expert", None, None),
        P("expert", None, None),
    )
    out_specs = (
        P(("dp", "expert"), None),
        P(("dp", "expert"), None),
        P("expert", "dp", None),
        P("expert", None, "dp"),
    )
    return jax.shard_map(shards, mesh=mesh, in_specs=in_specs, out_specs=out_specs, check_vma=False)
```

profile of v0, /device:TPU:0, one launch (start us, length us, event | category | flops | bytes accessed | tf_op | source)
XLA Modules:
  0.0 124.0 jit_solution(15628455643161868855)
XLA Ops:
  3.2 2.1 %fusion.15 = bf16[16,8,2048]{2,1,0:T(8,128)(2,1)} fusion(bf16[128,2048]{1,0:T(8,128)(2,1)} %param.6, s32[128]{0:T(128)S(1)} %compare_select_fusion), kind=kOutput, calls=%fused_computation.19 | convolution fusion | flops 67387392 | bytes 1049088 | tf_op jit(solution)/shard_map/dot_general | solution.py:20
  5.3 7.4 %all-to-all-start = ((bf16[16,8,2048]{2,1,0:T(8,128)(2,1)}), bf16[16,8,2048]{2,1,0:T(8,128)(2,1)}, u32[]{:S(2)}, u32[]{:S(2)}) async-start(bf16[16,8,2048]{2,1,0:T(8,128)(2,1)} %fusion.15), calls=%async_computation | async-start | bytes 1048576 | tf_op jit(solution)/shard_map/all_to_all | solution.py:27
  12.8 2.2 %fusion.16 = bf16[16,8,2048]{2,1,0:T(8,128)(2,1)} fusion(bf16[128,2048]{1,0:T(8,128)(2,1)} %param.9, f32[128]{0:T(128)} %param.8, s32[128]{0:T(128)S(1)} %compare_select_fusion), kind=kOutput, calls=%fused_computation.20 | convolution fusion | flops 68173824 | bytes 1049600 | tf_op jit(solution)/shard_map/dot_general | solution.py:22
  15.0 12.3 %all-to-all-done = bf16[16,8,2048]{2,1,0:T(8,128)(2,1)} async-done(((bf16[16,8,2048]{2,1,0:T(8,128)(2,1)}), bf16[16,8,2048]{2,1,0:T(8,128)(2,1)}, u32[]{:S(2)}, u32[]{:S(2)}) %all-to-all-start) | async-done | bytes 524320 | tf_op jit(solution)/shard_map/all_to_all | solution.py:27
  27.3 4.2 %all-to-all-start.2 = ((bf16[16,8,2048]{2,1,0:T(8,128)(2,1)}), bf16[16,8,2048]{2,1,0:T(8,128)(2,1)}, u32[]{:S(2)}, u32[]{:S(2)}) async-start(bf16[16,8,2048]{2,1,0:T(8,128)(2,1)} %fusion.16), calls=%async_computation.2 | async-start | bytes 1048576 | tf_op jit(solution)/shard_map/all_to_all | solution.py:39
  31.6 2.2 %all_to_all.40 = bf16[128,2,1024]{2,1,0:T(2,128)(2,1)} reshape(bf16[16,8,2048]{2,1,0:T(8,128)(2,1)} %all-to-all-done) | data formatting | bytes 1048576 | tf_op jit(solution)/shard_map/all_to_all | solution.py:69
  35.8 10.2 %all-to-all-done.2 = bf16[16,8,2048]{2,1,0:T(8,128)(2,1)} async-done(((bf16[16,8,2048]{2,1,0:T(8,128)(2,1)}), bf16[16,8,2048]{2,1,0:T(8,128)(2,1)}, u32[]{:S(2)}, u32[]{:S(2)}) %all-to-all-start.2) | async-done | bytes 524320 | tf_op jit(solution)/shard_map/all_to_all | solution.py:39
  46.0 4.2 %all-to-all-start.4 = ((bf16[128,2,1024]{0,2,1:T(8,128)(2,1)}), bf16[128,2,1024]{0,2,1:T(8,128)(2,1)}, u32[]{:S(2)}, u32[]{:S(2)}) async-start(bf16[128,2,1024]{0,2,1:T(8,128)(2,1)} %copy.12), calls=%async_computation.4 | async-start | bytes 1048576 | tf_op jit(solution)/shard_map/all_to_all | solution.py:69
  50.2 2.2 %all_to_all.43 = bf16[128,2,1024]{2,1,0:T(2,128)(2,1)} reshape(bf16[16,8,2048]{2,1,0:T(8,128)(2,1)} %all-to-all-done.2) | data formatting | bytes 1048576 | tf_op jit(solution)/shard_map/all_to_all | solution.py:70
  52.5 2.1 %copy.13 = bf16[128,2,1024]{2,0,1:T(8,128)(2,1)} copy(bf16[128,2,1024]{2,1,0:T(2,128)(2,1)} %all_to_all.43) | data formatting | bytes 1048576 | tf_op jit(solution)/shard_map/all_to_all | solution.py:70
  56.3 2.2 %fusion.29 = bf16[128,768]{1,0:T(8,128)(2,1)S(1)} fusion(bf16[1,768,2048]{2,1,0:T(8,128)(2,1)S(1)} %copy-done.2, bf16[16,8,2048]{2,1,0:T(8,128)(2,1)} %all-to-all-done.2, f32[128,768]{1,0:T(8,128)S(1)} %get-tuple-element.5), kind=kOutput, calls=%fused_computation.25 | convolution fusion | flops 403537920 | bytes 4259840 | tf_op jit(solution)/shard_map/dot_general | solution.py:41
  58.8 4.2 %all-to-all-start.5 = ((bf16[128,2,1024]{2,0,1:T(8,128)(2,1)}), bf16[128,2,1024]{2,0,1:T(8,128)(2,1)}, u32[]{:S(2)}, u32[]{:S(2)}) async-start(bf16[128,2,1024]{2,0,1:T(8,128)(2,1)} %copy.13), calls=%async_computation.5 | async-start | bytes 1048576 | tf_op jit(solution)/shard_map/all_to_all | solution.py:70
  64.9 6.4 %all-to-all-done.5 = bf16[128,2,1024]{2,0,1:T(8,128)(2,1)} async-done(((bf16[128,2,1024]{2,0,1:T(8,128)(2,1)}), bf16[128,2,1024]{2,0,1:T(8,128)(2,1)}, u32[]{:S(2)}, u32[]{:S(2)}) %all-to-all-start.5) | async-done | bytes 524320 | tf_op jit(solution)/shard_map/all_to_all | solution.py:70
  71.3 4.4 %all-to-all-start.3 = ((bf16[16,8,2048]{2,1,0:T(8,128)(2,1)}), bf16[16,8,2048]{2,1,0:T(8,128)(2,1)}, u32[]{:S(2)}, u32[]{:S(2)}) async-start(bf16[16,8,2048]{2,1,0:T(8,128)(2,1)} %fusion.20), calls=%async_computation.3 | async-start | bytes 1048576 | tf_op jit(solution)/shard_map/all_to_all | solution.py:54
  75.7 7.8 %all_gather.6 = bf16[256,768]{1,0:T(8,128)(2,1)S(1)} all-gather(bf16[128,768]{1,0:T(8,128)(2,1)S(1)} %fusion.29), channel_id=1, replica_groups=mesh['dp'=2,'expert'=16] {'dp'}, dimensions={0}, use_global_device_ids=true | all-gather | bytes 589824 | tf_op jit(solution)/shard_map/all_gather | solution.py:73
  83.5 7.1 %all_gather.7 = bf16[256,768]{1,0:T(8,128)(2,1)S(1)} all-gather(bf16[128,768]{1,0:T(8,128)(2,1)S(1)} %get-tuple-element.4), channel_id=1, replica_groups=mesh['dp'=2,'expert'=16] {'dp'}, dimensions={0}, use_global_device_ids=true | all-gather | bytes 589824 | tf_op jit(solution)/shard_map/all_gather | solution.py:72
  90.6 3.3 %fusion.17 = bf16[16,8,2048]{2,1,0:T(8,128)(2,1)} fusion(bf16[128,768]{1,0:T(8,128)(2,1)S(1)} %get-tuple-element.4, bf16[1,768,2048]{2,1,0:T(8,128)(2,1)} %param.11), kind=kOutput, calls=%fused_computation.21 | convolution fusion | flops 402915328 | bytes 3866624 | tf_op jit(solution)/shard_map/dot_general | solution.py:31
  93.9 3.9 %convert_reduce_fusion = f32[768,1024]{1,0:T(8,128)} fusion(bf16[2,128,768]{2,1,0:T(8,128)(2,1)S(1)} %bitcast.66, bf16[128,2,1024]{2,0,1:T(8,128)(2,1)} %all-to-all-done.5), kind=kOutput, calls=%fused_computation | convolution fusion | flops 406585344 | bytes 4063232 | tf_op jit(solution)/shard_map/krf,krw->kfw/dot_general | solution.py:82
  97.8 3.9 %convert_reduce_fusion.1 = f32[1024,768]{1,0:T(8,128)} fusion(bf16[2,128,768]{2,1,0:T(8,128)(2,1)S(1)} %bitcast.65, bf16[128,2,1024]{0,2,1:T(8,128)(2,1)} %all-to-all-done.4), kind=kOutput, calls=%fused_computation.1 | convolution fusion | flops 406585344 | bytes 4063232 | tf_op jit(solution)/shard_map/krw,krf->kwf/dot_general | solution.py:81
  101.7 5.6 %all-to-all-start.1 = ((bf16[16,8,2048]{2,1,0:T(8,128)(2,1)}), bf16[16,8,2048]{2,1,0:T(8,128)(2,1)}, u32[]{:S(2)}, u32[]{:S(2)}) async-start(bf16[16,8,2048]{2,1,0:T(8,128)(2,1)} %fusion.17), calls=%async_computation.1 | async-start | bytes 1048576 | tf_op jit(solution)/shard_map/all_to_all | solution.py:38
  107.3 3.9 %multiply_bitcast_fusion.1 = f32[1,1024,768]{2,1,0:T(8,128)} fusion(f32[1024,768]{1,0:T(8,128)} %convert_reduce_fusion.1), kind=kLoop, calls=%fused_computation.11 | loop fusion | flops 786432 | bytes 6291456 | tf_op jit(solution)/shard_map/mul | solution.py:92
  113.2 2.2 %convolution_convert_fusion = bf16[128,2048]{1,0:T(8,128)(2,1)} fusion(bf16[16,8,2048]{2,1,0:T(8,128)(2,1)} %all-to-all-done.3, s32[128]{0:T(128)S(1)} %compare_select_fusion), kind=kOutput, calls=%fused_computation.16 | convolution fusion | flops 67387392 | bytes 1049088 | tf_op jit(solution)/shard_map/dot_general | solution.py:59
  115.4 6.4 %all-to-all-done.1 = bf16[16,8,2048]{2,1,0:T(8,128)(2,1)} async-done(((bf16[16,8,2048]{2,1,0:T(8,128)(2,1)}), bf16[16,8,2048]{2,1,0:T(8,128)(2,1)}, u32[]{:S(2)}, u32[]{:S(2)}) %all-to-all-start.1) | async-done | bytes 524320 | tf_op jit(solution)/shard_map/all_to_all | solution.py:38
  121.8 2.2 %fusion.8 = bf16[128,2048]{1,0:T(8,128)(2,1)} fusion(bf16[16,8,2048]{2,1,0:T(8,128)(2,1)} %all-to-all-done.1, f32[128]{0:T(128)S(1)} %copy-done.3, s32[128]{0:T(128)S(1)} %compare_select_fusion), kind=kOutput, calls=%fused_computation.13 | convolution fusion | flops 67649536 | bytes 1049600 | tf_op jit(solution)/shard_map/dot_general | solution.py:56
  (18 shorter events, 10.4 us)
Async XLA Ops:
  0.6 53.9 %copy-start = (bf16[1,2048,768]{2,1,0:T(8,128)(2,1)S(1)}, bf16[1,2048,768]{2,1,0:T(8,128)(2,1)}, u32[]{:S(2)}) copy-start(bf16[1,2048,768]{2,1,0:T(8,128)(2,1)} %param.10) | copy-start | bytes 9437188
  5.3 22.0 %all-to-all-start = ((bf16[16,8,2048]{2,1,0:T(8,128)(2,1)}), bf16[16,8,2048]{2,1,0:T(8,128)(2,1)}, u32[]{:S(2)}, u32[]{:S(2)}) async-start(bf16[16,8,2048]{2,1,0:T(8,128)(2,1)} %fusion.15), calls=%async_computation | async-start | bytes 1048576 | tf_op jit(solution)/shard_map/all_to_all | solution.py:27
  27.3 18.7 %all-to-all-start.2 = ((bf16[16,8,2048]{2,1,0:T(8,128)(2,1)}), bf16[16,8,2048]{2,1,0:T(8,128)(2,1)}, u32[]{:S(2)}, u32[]{:S(2)}) async-start(bf16[16,8,2048]{2,1,0:T(8,128)(2,1)} %fusion.16), calls=%async_computation.2 | async-start | bytes 1048576 | tf_op jit(solution)/shard_map/all_to_all | solution.py:39
  46.0 12.7 %all-to-all-start.4 = ((bf16[128,2,1024]{0,2,1:T(8,128)(2,1)}), bf16[128,2,1024]{0,2,1:T(8,128)(2,1)}, u32[]{:S(2)}, u32[]{:S(2)}) async-start(bf16[128,2,1024]{0,2,1:T(8,128)(2,1)} %copy.12), calls=%async_computation.4 | async-start | bytes 1048576 | tf_op jit(solution)/shard_map/all_to_all | solution.py:69
  52.5 3.8 %copy-start.2 = (bf16[1,768,2048]{2,1,0:T(8,128)(2,1)S(1)}, bf16[1,768,2048]{2,1,0:T(8,128)(2,1)}, u32[]{:S(2)}) copy-start(bf16[1,768,2048]{2,1,0:T(8,128)(2,1)} %param.11) | copy-start | bytes 9437188
  58.8 12.5 %all-to-all-start.5 = ((bf16[128,2,1024]{2,0,1:T(8,128)(2,1)}), bf16[128,2,1024]{2,0,1:T(8,128)(2,1)}, u32[]{:S(2)}, u32[]{:S(2)}) async-start(bf16[128,2,1024]{2,0,1:T(8,128)(2,1)} %copy.13), calls=%async_computation.5 | async-start | bytes 1048576 | tf_op jit(solution)/shard_map/all_to_all | solution.py:70
  71.3 30.4 %all-to-all-start.3 = ((bf16[16,8,2048]{2,1,0:T(8,128)(2,1)}), bf16[16,8,2048]{2,1,0:T(8,128)(2,1)}, u32[]{:S(2)}, u32[]{:S(2)}) async-start(bf16[16,8,2048]{2,1,0:T(8,128)(2,1)} %fusion.20), calls=%async_computation.3 | async-start | bytes 1048576 | tf_op jit(solution)/shard_map/all_to_all | solution.py:54
  101.7 20.1 %all-to-all-start.1 = ((bf16[16,8,2048]{2,1,0:T(8,128)(2,1)}), bf16[16,8,2048]{2,1,0:T(8,128)(2,1)}, u32[]{:S(2)}, u32[]{:S(2)}) async-start(bf16[16,8,2048]{2,1,0:T(8,128)(2,1)} %fusion.17), calls=%async_computation.1 | async-start | bytes 1048576 | tf_op jit(solution)/shard_map/all_to_all | solution.py:38
  107.3 3.9 %copy-start.1 = (f32[768,1024]{1,0:T(8,128)S(1)}, f32[768,1024]{1,0:T(8,128)}, u32[]{:S(2)}) copy-start(f32[768,1024]{1,0:T(8,128)} %convert_reduce_fusion) | copy-start | bytes 9437188
  111.2 10.6 %copy-start.3 = (f32[128]{0:T(128)S(1)}, f32[128]{0:T(128)}, u32[]{:S(2)}) copy-start(f32[128]{0:T(128)} %param.8) | copy-start | bytes 1540
where the time goes:
time: 125 us; the launch traced here: 124 us
  waiting for transfers between devices  35.6 us (28%)
  starting transfers between devices  30.1 us (24%)
  matrix products  25.6 us (20%)
  blocking collectives  15 us (12%)
  local copies, waits for them, and re-layouts  8.57 us (7%)
  other arithmetic  8.44 us (7%)
    all_to_all x1, waiting for transfers between devices, shards(): lax.all_to_all(send_x, 'expert', split_axis=0, concat_axis=0, tiled=True)  12.3 us
    all_to_all x1, waiting for transfers between devices, shards(): lax.all_to_all(send_c, 'expert', split_axis=0, concat_axis=0, tiled=True)  10.2 us
    all_gather x1, blocking collectives, shards(): grad_piece = lax.all_gather(grad_pre, 'dp', axis=0, tiled=True)  7.83 us
    all_to_all x1, starting transfers between devices, shards(): lax.all_to_all(send_x, 'expert', split_axis=0, concat_axis=0, tiled=True)  7.44 us
    all_gather x1, blocking collectives, shards(): hidden_piece = lax.all_gather(hidden, 'dp', axis=0, tiled=True)  7.12 us
    all_to_all x1, waiting for transfers between devices, shards(): lax.all_to_all(expert_out, 'expert', split_axis=0, concat_axis=0, tiled=T...  6.44 us
    all_to_all x1, waiting for transfers between devices, shards(): lax.all_to_all(rows_c, 'dp', split_axis=1, concat_axis=0, tiled=True)  6.37 us
    mul x2, other arithmetic, shards(): return (layer_out, token_grad, sum_up * inverse, sum_down * inverse)  5.89 us
  transfers between devices with their start and end apart: 6, of which 5 were waited for; matrix products, arithmetic and copies ran while one was open for 25% of the time, Pallas kernels for 0%

commit v1 on v0

v1 whole, which is shorter than its diff:
```python
import functools

import jax
import jax.numpy as jnp
from jax import lax
from jax.experimental import pallas as pl
from jax.experimental.pallas import tpu as pltpu
from jax.sharding import PartitionSpec as P

MESH = pl.DeviceIdType.MESH
F32 = jnp.float32
BF16 = jnp.bfloat16
CHUNK = 4


def column(row):
    t = row.shape[1]
    eye = lax.broadcasted_iota(jnp.int32, (t, t), 0) == lax.broadcasted_iota(jnp.int32, (t, t), 1)
    return jnp.sum(jnp.where(eye, row, jnp.zeros_like(row)), axis=1, keepdims=True)


def place(ids, me, n, capacity):
    t = ids.shape[1]
    onehot = lax.broadcasted_iota(jnp.int32, (n, t), 0) == ids
    before = lax.broadcasted_iota(jnp.int32, (t, t), 0) < lax.broadcasted_iota(jnp.int32, (t, t), 1)
    counts = jnp.dot(
        onehot.astype(F32).astype(BF16), before.astype(F32).astype(BF16), preferred_element_type=F32
    )
    rank = jnp.sum(jnp.where(onehot, counts, 0.0), axis=0, keepdims=True).astype(jnp.int32)
    offset = ids - me
    offset = jnp.where(offset < 0, offset + n, offset)
    return offset, rank, rank < capacity


def exchange_kernel(
    n, groups, capacity, pad, ids_ref, gate_ref, tokens_ref, cot_ref, wup_hbm, wdn_hbm,
    back_ref, a_all, hg_all, wup, wdn, send, recv, ret, hg,
    w_sem, send_sem, recv_sem, rsend_sem, rrecv_sem, self_sem,
    a_sem, h_sem, asend_sem, arecv_sem, hsend_sem, hrecv_sem,
):
    dp = lax.axis_index("dp")
    me = lax.axis_index("expert")
    width = tokens_ref.shape[1]
    units = wup.shape[1]
    cols = width // groups
    chunks = n // CHUNK
    wcopy = [
        pltpu.make_async_copy(wup_hbm, wup, w_sem.at[0]),
        pltpu.make_async_copy(wdn_hbm, wdn, w_sem.at[1]),
    ]
    for copy in wcopy:
        copy.start()

    barrier = pltpu.get_barrier_semaphore()

    @pl.loop(1, n)
    def _(k):
        pl.semaphore_signal(
            barrier, inc=1, device_id=(dp, lax.rem(me + k, n)), device_id_type=MESH
        )

    @pl.loop(1, groups)
    def _(d):
        pl.semaphore_signal(
            barrier, inc=1, device_id=(lax.rem(dp + d, groups), me), device_id_type=MESH
        )

    offset, rank, kept = place(ids_ref[...], me, n, capacity)
    t = tokens_ref.shape[0]
    target = jnp.where(kept, offset * pad + rank, -1)
    select = (lax.broadcasted_iota(jnp.int32, (n * pad, t), 0) == target).astype(F32).astype(BF16)
    scaled = (column(gate_ref[...]) * cot_ref[...].astype(F32)).astype(BF16)
    step = 512 if width % 512 == 0 else width
    for at in range(0, width, step):
        x = jnp.dot(select, tokens_ref[:, at : at + step], preferred_element_type=F32)
        c = jnp.dot(select, scaled[:, at : at + step], preferred_element_type=F32)
        both = jnp.concatenate([x.reshape(n, pad, step), c.reshape(n, pad, step)], axis=1)
        both = both.astype(BF16)
        send[:, :, at : at + step] = both
        recv[0, :, at : at + step] = both[0]

    pl.semaphore_wait(barrier, n - 1 + groups - 1)

    def forth(k):
        return pltpu.make_async_remote_copy(
            src_ref=send.at[k], dst_ref=recv.at[k], send_sem=send_sem.at[k],
            recv_sem=recv_sem.at[k], device_id=(dp, lax.rem(me + k, n)), device_id_type=MESH,
        )

    def home(k):
        return pltpu.make_async_remote_copy(
            src_ref=ret.at[k], dst_ref=back_ref.at[k], send_sem=rsend_sem.at[k],
            recv_sem=rrecv_sem.at[k], device_id=(dp, lax.rem(me + n - k, n)), device_id_type=MESH,
        )

    def a_local(c):
        return pltpu.make_async_copy(
            recv.at[pl.ds(c * CHUNK, CHUNK), :, pl.ds(pl.multiple_of(dp * cols, 128), cols)],
            a_all.at[0, pl.ds(c * CHUNK, CHUNK)], a_sem.at[c],
        )

    def h_local(c):
        return pltpu.make_async_copy(
            hg.at[pl.ds(c * CHUNK, CHUNK)], hg_all.at[0, pl.ds(c * CHUNK, CHUNK)], h_sem.at[c]
        )

    def a_remote(c, d):
        peer = lax.rem(dp + d, groups)
        return pltpu.make_async_remote_copy(
            src_ref=recv.at[
                pl.ds(c * CHUNK, CHUNK), :, pl.ds(pl.multiple_of(peer * cols, 128), cols)
            ],
            dst_ref=a_all.at[d, pl.ds(c * CHUNK, CHUNK)], send_sem=asend_sem.at[d, c],
            recv_sem=arecv_sem.at[d, c], device_id=(peer, me), device_id_type=MESH,
        )

    def h_remote(c, d):
        peer = lax.rem(dp + d, groups)
        return pltpu.make_async_remote_copy(
            src_ref=hg.at[pl.ds(c * CHUNK, CHUNK)],
            dst_ref=hg_all.at[d, pl.ds(c * CHUNK, CHUNK)], send_sem=hsend_sem.at[d, c],
            recv_sem=hrecv_sem.at[d, c], device_id=(peer, me), device_id_type=MESH,
        )

    @pl.loop(1, n)
    def _(i):
        forth(n - i).start()

    for copy in wcopy:
        copy.wait()

    rows = CHUNK * pad
    nt = (((1,), (1,)), ((), ()))

    @pl.loop(0, chunks)
    def _(i):
        c = chunks - 1 - i

        @pl.loop(0, CHUNK)
        def _(j):
            k = c * CHUNK + j

            @pl.when(k > 0)
            def _():
                forth(k).wait_recv()

        a_local(c).start()

        @pl.loop(1, groups)
        def _(d):
            a_remote(c, d).start()

        a = recv[pl.ds(c * CHUNK, CHUNK)].reshape(2 * rows, width)
        pre = jnp.dot(a, wup[...], preferred_element_type=F32)
        grad = lax.dot_general(a, wdn[...], nt, preferred_element_type=F32)
        pre = pre.reshape(CHUNK, 2, pad, units)[:, 0]
        grad = grad.reshape(CHUNK, 2, pad, units)[:, 1]
        sigma = 1.0 / (1.0 + jnp.exp(-pre))
        hidden = pre * sigma
        grad = grad * sigma * (1.0 + pre * (1.0 - sigma))
        hg[pl.ds(c * CHUNK, CHUNK)] = jnp.concatenate([grad, hidden], axis=1).astype(BF16)
        h_local(c).start()

        @pl.loop(1, groups)
        def _(d):
            h_remote(c, d).start()

        hidden = hidden.reshape(rows, units).astype(BF16)
        grad = grad.reshape(rows, units).astype(BF16)
        for at in range(0, width, step):
            out = jnp.dot(hidden, wdn[:, at : at + step], preferred_element_type=F32)
            tok = lax.dot_general(grad, wup[at : at + step, :], nt, preferred_element_type=F32)
            both = jnp.concatenate(
                [tok.reshape(CHUNK, pad, step), out.reshape(CHUNK, pad, step)], axis=1
            )
            ret[pl.ds(c * CHUNK, CHUNK), :, at : at + step] = both.astype(BF16)

        @pl.loop(0, CHUNK)
        def _(j):
            k = c * CHUNK + j

            @pl.when(k > 0)
            def _():
                home(k).start()

    own = pltpu.make_async_copy(ret.at[0], back_ref.at[0], self_sem)
    own.start()

    @pl.loop(0, chunks)
    def _(c):
        a_local(c).wait()
        h_local(c).wait()

        @pl.loop(1, groups)
        def _(d):
            a_remote(c, d).wait()
            h_remote(c, d).wait()

    @pl.loop(1, n)
    def _(k):
        forth(k).wait_send()
        home(k).wait()

    own.wait()


def exchange(n, groups, capacity, pad, ids, gate, tokens, cot, wup, wdn):
    width = tokens.shape[1]
    units = wup.shape[1]
    chunks = n // CHUNK
    vmem = pl.BlockSpec(memory_space=pltpu.VMEM)
    hbm = pl.BlockSpec(memory_space=pl.ANY)
    dma = pltpu.SemaphoreType.DMA
    block = (n, 2 * pad, width)
    return pl.pallas_call(
        functools.partial(exchange_kernel, n, groups, capacity, pad),
        out_shape=(
            jax.ShapeDtypeStruct(block, BF16),
            jax.ShapeDtypeStruct((groups, n, 2 * pad, width // groups), BF16),
            jax.ShapeDtypeStruct((groups, n, 2 * pad, units), BF16),
        ),
        in_specs=[vmem, vmem, vmem, vmem, hbm, hbm],
        out_specs=(hbm, hbm, hbm),
        scratch_shapes=[
            pltpu.VMEM(wup.shape, BF16), pltpu.VMEM(wdn.shape, BF16),
            pltpu.VMEM(block, BF16), pltpu.VMEM(block, BF16), pltpu.VMEM(block, BF16),
            pltpu.VMEM((n, 2 * pad, units), BF16),
            dma((2,)), dma((n,)), dma((n,)), dma((n,)), dma((n,)), dma,
            dma((chunks,)), dma((chunks,)),
            dma((groups, chunks)), dma((groups, chunks)),
            dma((groups, chunks)), dma((groups, chunks)),
        ],
        compiler_params=pltpu.CompilerParams(
            collective_id=0, has_side_effects=True, vmem_limit_bytes=44 * 2**20
        ),
        name="expert_exchange",
    )(ids, gate, tokens, cot, wup, wdn)


def finish_kernel(
    n, capacity, pad, inverse, me_ref, ids_ref, gate_ref, back_ref, a_ref, hg_ref,
    out_ref, tok_ref, up_ref, down_ref,
):
    g = pl.program_id(1)

    @pl.when(g == 0)
    def _():
        offset, rank, kept = place(ids_ref[...], me_ref[0, 0], n, capacity)
        target = column(jnp.where(kept, offset * (2 * pad) + rank, -2 * pad))
        t = target.shape[0]
        slot = lax.broadcasted_iota(jnp.int32, (t, n * 2 * pad), 1)
        pick_tok = (slot == target).astype(F32).astype(BF16)
        pick_out = (slot == target + pad).astype(F32).astype(BF16)
        rows = back_ref[...]
        tok_ref[...] = jnp.dot(pick_tok, rows, preferred_element_type=F32).astype(BF16)
        out = jnp.dot(pick_out, rows, preferred_element_type=F32)
        out_ref[...] = (column(gate_ref[...]) * out).astype(BF16)

    a = a_ref[0]
    hg = hg_ref[0]
    first = lax.rem(lax.broadcasted_iota(jnp.int32, hg.shape, 0), 2 * pad) < pad
    zero = jnp.zeros_like(hg)
    tn = (((0,), (0,)), ((), ()))
    up = lax.dot_general(a, jnp.where(first, hg, zero), tn, preferred_element_type=F32) * inverse
    down = lax.dot_general(jnp.where(first, zero, hg), a, tn, preferred_element_type=F32) * inverse

    @pl.when(g == 0)
    def _():
        up_ref[...] = up
        down_ref[...] = down

    @pl.when(g > 0)
    def _():
        up_ref[...] += up
        down_ref[...] += down


def finish(n, groups, capacity, pad, me, ids, gate, back, a_all, hg_all):
    rows, cols = a_all.shape[1], a_all.shape[2]
    units = hg_all.shape[2]
    t = ids.shape[1]
    width = back.shape[1]
    tile = 256 if cols % 256 == 0 else cols
    tiles = cols // tile
    wide = width // tiles
    whole = pl.BlockSpec((1, t), lambda j, g: (0, 0))
    return pl.pallas_call(
        functools.partial(finish_kernel, n, capacity, pad, 1.0 / groups),
        grid=(tiles, groups),
        out_shape=(
            jax.ShapeDtypeStruct((t, width), BF16),
            jax.ShapeDtypeStruct((t, width), BF16),
            jax.ShapeDtypeStruct((cols, units), F32),
            jax.ShapeDtypeStruct((units, cols), F32),
        ),
        in_specs=[
            pl.BlockSpec(memory_space=pltpu.SMEM),
            whole,
            whole,
            pl.BlockSpec((rows, wide), lambda j, g: (0, j)),
            pl.BlockSpec((1, rows, tile), lambda j, g: (g, 0, j)),
            pl.BlockSpec((1, rows, units), lambda j, g: (g, 0, 0)),
        ],
        out_specs=(
            pl.BlockSpec((t, wide), lambda j, g: (0, j)),
            pl.BlockSpec((t, wide), lambda j, g: (0, j)),
            pl.BlockSpec((tile, units), lambda j, g: (j, 0)),
            pl.BlockSpec((units, tile), lambda j, g: (0, j)),
        ),
        compiler_params=pltpu.CompilerParams(vmem_limit_bytes=40 * 2**20),
        name="finish",
    )(me, ids, gate, back, a_all, hg_all)


def shards(tokens, expert_ids, gate, cotangent, w_up, w_down):
    t = tokens.shape[0]
    n = lax.axis_size("expert")
    groups = lax.axis_size("dp")
    capacity = t // n
    pad = -(-capacity // 8) * 8
    ids = expert_ids[None]
    gate = gate[None]
    back, a_all, hg_all = exchange(
        n, groups, capacity, pad, ids, gate, tokens, cotangent, w_up[0], w_down[0]
    )
    me = lax.axis_index("expert").astype(jnp.int32).reshape(1, 1)
    rows = n * 2 * pad
    out, tok, up, down = finish(
        n, groups, capacity, pad, me, ids, gate, back.reshape(rows, -1),
        a_all.reshape(groups, rows, -1), hg_all.reshape(groups, rows, -1),
    )
    return out, tok, up[None], down[None]


def solution(mesh):
    in_specs = (
        P(("dp", "expert"), None),
        P(("dp", "expert")),
        P(("dp", "expert")),
        P(("dp", "expert"), None),
        P("expert", None, None),
        P("expert", None, None),
    )
    out_specs = (
        P(("dp", "expert"), None),
        P(("dp", "expert"), None),
        P("expert", "dp", None),
        P("expert", None, "dp"),
    )
    return jax.shard_map(shards, mesh=mesh, in_specs=in_specs, out_specs=out_specs, check_vma=False)
```

time: 125 us -> 73.7 us (0.59)
  Pallas kernels: 0 us -> 65.6 us
  waiting for transfers between devices: 35.6 us -> 0 us
  starting transfers between devices: 30.1 us -> 0 us
  matrix products: 25.6 us -> 0 us
  blocking collectives: 15 us -> 0 us
  other arithmetic: 8.44 us -> 0 us
  local copies, waits for them, and re-layouts: 8.57 us -> 7.16 us
    pallas_call x0 -> x2, Pallas kernels: none -> 65.6 us  [the longest x1 57.2 us: exchange(): pl.pallas_call(functools.partial(exchange_kernel, n, groups, capacity, pa...]
    all_to_all x6 -> x0, waiting for transfers between devices: 35.6 us -> none  [the longest x1 12.3 us: shards(): lax.all_to_all(send_x, 'expert', split_axis=0, concat_axis=0, tiled=True)]
    all_to_all x6 -> x0, starting transfers between devices: 30.1 us -> none  [the longest x1 7.44 us: shards(): lax.all_to_all(send_x, 'expert', split_axis=0, concat_axis=0, tiled=True)]
    dot_general x10 -> x0, matrix products: 25.6 us -> none  [the longest x1 3.92 us: shards(): jnp.einsum('krf,krw->kfw', hidden_piece, part_c, preferred_element_type=j...]
    all_gather x2 -> x0, blocking collectives: 15 us -> none  [the longest x1 7.83 us: shards(): grad_piece = lax.all_gather(grad_pre, 'dp', axis=0, tiled=True)]
    all_to_all x4 -> x0, local copies, waits for them, and re-layouts: 8.55 us -> none  [the longest x2 4.32 us: shards(): lax.all_to_all(rows_c, 'dp', split_axis=1, concat_axis=0, tiled=True)]
    unnamed x8 -> x12, local copies, waits for them, and re-layouts: 0.02 us -> 7.16 us
    mul x2 -> x0, other arithmetic: 5.89 us -> none  [shards(): return (layer_out, token_grad, sum_up * inverse, sum_down * inverse)]
  transfers between devices with their start and end apart: 6 -> 0, of which waited for: 5 -> 0; matrix products, arithmetic and copies ran while one was open for 25% -> 0% of each run, Pallas kernels for 0% -> 0%
where the time goes in v1:
time: 73.7 us; the launch traced here: 73.4 us
  Pallas kernels  65.6 us (89%)
  local copies, waits for them, and re-layouts  7.16 us (10%)
    pallas_call x1, Pallas kernels, exchange(): pl.pallas_call(functools.partial(exchange_kernel, n, groups, capacity, pa...  57.2 us
    pallas_call x1, Pallas kernels, finish(): pl.pallas_call(functools.partial(finish_kernel, n, capacity, pad, 1.0 / g...  8.45 us
    unnamed x12, local copies, waits for them, and re-layouts  7.16 us

profile of v1, /device:TPU:0, one launch (start us, length us, event | category | flops | bytes accessed | tf_op | source)
XLA Modules:
  0.0 73.4 jit_solution(12173770177740813581)
XLA Ops:
  0.6 0.0 copy-start
  0.6 1.9 %copy-done = bf16[1,2048,768]{2,1,0:T(8,128)(2,1)S(1)} copy-done((bf16[1,2048,768]{2,1,0:T(8,128)(2,1)S(1)}, bf16[1,2048,768]{2,1,0:T(8,128)(2,1)}, u32[]{:S(2)}) %copy-start) | copy-done | bytes 3145752
  2.5 0.0 copy-start.1
  2.5 1.9 %copy-done.1 = bf16[1,768,2048]{2,1,0:T(8,128)(2,1)S(1)} copy-done((bf16[1,768,2048]{2,1,0:T(8,128)(2,1)S(1)}, bf16[1,768,2048]{2,1,0:T(8,128)(2,1)}, u32[]{:S(2)}) %copy-start.1) | copy-done | bytes 3145752
  4.4 0.0 copy-start.2
  4.4 1.0 %copy-done.2 = bf16[128,2048]{1,0:T(8,128)(2,1)S(1)} copy-done((bf16[128,2048]{1,0:T(8,128)(2,1)S(1)}, bf16[128,2048]{1,0:T(8,128)(2,1)}, u32[]{:S(2)}) %copy-start.2) | copy-done | bytes 524312
  5.5 0.0 copy-start.3
  5.5 1.0 %copy-done.3 = bf16[128,2048]{1,0:T(8,128)(2,1)S(1)} copy-done((bf16[128,2048]{1,0:T(8,128)(2,1)S(1)}, bf16[128,2048]{1,0:T(8,128)(2,1)}, u32[]{:S(2)}) %copy-start.3) | copy-done | bytes 524312
  6.5 0.0 copy-start.4
  6.5 0.7 copy-done.4
  7.2 0.0 copy-start.5
  7.2 0.7 copy-done.5
  7.8 57.2 %expert_exchange.1 = (bf16[16,16,2048]{2,1,0:T(8,128)(2,1)S(1)}, bf16[2,16,16,1024]{3,2,1,0:T(8,128)(2,1)S(1)}, bf16[2,16,16,768]{3,2,1,0:T(8,128)(2,1)S(1)}) custom-call(s32[1,128]{1,0:T(1,128)S(1)} %bitcast.15, f32[1,128]{1,0:T(1,128)S(1)} %bitcast.17, bf16[128,2048]{1,0:T(8,128)(2,1)S(1)} %copy-done.2, bf16[128,2048]{1,0:T(8,128)(2,1)S(1)} %copy-done.3, ...), custom_call_target="tpu_custom_call" | custom-call | tf_op jit(solution)/shard_map/expert_exchange/pallas_call | solution.py:215
  65.0 8.4 %finish.1 = (bf16[128,2048]{1,0:T(8,128)(2,1)}, bf16[128,2048]{1,0:T(8,128)(2,1)}, f32[1024,768]{1,0:T(8,128)}, f32[768,1024]{1,0:T(8,128)}) custom-call(s32[1,1]{1,0:T(1,128)} %bitcast.me_ref, s32[1,128]{1,0:T(1,128)S(1)} %bitcast.16, f32[1,128]{1,0:T(1,128)S(1)} %bitcast.18, bf16[256,2048]{1,0:T(8,128)(2,1)S(1)} %bitcast.12, ...), custom_call_target="tpu_custom_call" | custom-call | tf_op jit(solution)/shard_map/finish/pallas_call | solution.py:287
Async XLA Ops:
  0.6 1.9 %copy-start = (bf16[1,2048,768]{2,1,0:T(8,128)(2,1)S(1)}, bf16[1,2048,768]{2,1,0:T(8,128)(2,1)}, u32[]{:S(2)}) copy-start(bf16[1,2048,768]{2,1,0:T(8,128)(2,1)} %param.10) | copy-start | bytes 9437188
  2.5 1.9 %copy-start.1 = (bf16[1,768,2048]{2,1,0:T(8,128)(2,1)S(1)}, bf16[1,768,2048]{2,1,0:T(8,128)(2,1)}, u32[]{:S(2)}) copy-start(bf16[1,768,2048]{2,1,0:T(8,128)(2,1)} %param.11) | copy-start | bytes 9437188
  4.4 1.0 %copy-start.2 = (bf16[128,2048]{1,0:T(8,128)(2,1)S(1)}, bf16[128,2048]{1,0:T(8,128)(2,1)}, u32[]{:S(2)}) copy-start(bf16[128,2048]{1,0:T(8,128)(2,1)} %tokens_ref.1) | copy-start | bytes 1572868
  5.5 1.0 %copy-start.3 = (bf16[128,2048]{1,0:T(8,128)(2,1)S(1)}, bf16[128,2048]{1,0:T(8,128)(2,1)}, u32[]{:S(2)}) copy-start(bf16[128,2048]{1,0:T(8,128)(2,1)} %cot_ref.1) | copy-start | bytes 1572868
  6.5 0.7 copy-start.4
  7.2 0.7 copy-start.5

commit v2 on v1

v2 whole, which is shorter than its diff:
```python
import functools
import math

import jax
import jax.numpy as jnp
from jax import lax
from jax.experimental import pallas as pl
from jax.experimental.pallas import tpu as pltpu
from jax.sharding import PartitionSpec as P

MESH = pl.DeviceIdType.MESH
F32 = jnp.float32
BF16 = jnp.bfloat16
CHUNK = 4


def column(row):
    t = row.shape[1]
    eye = lax.broadcasted_iota(jnp.int32, (t, t), 0) == lax.broadcasted_iota(jnp.int32, (t, t), 1)
    return jnp.sum(jnp.where(eye, row, jnp.zeros_like(row)), axis=1, keepdims=True)


def place(ids, me, n, capacity):
    t = ids.shape[1]
    onehot = lax.broadcasted_iota(jnp.int32, (n, t), 0) == ids
    before = lax.broadcasted_iota(jnp.int32, (t, t), 0) < lax.broadcasted_iota(jnp.int32, (t, t), 1)
    counts = jnp.dot(
        onehot.astype(F32).astype(BF16), before.astype(F32).astype(BF16), preferred_element_type=F32
    )
    rank = jnp.sum(jnp.where(onehot, counts, 0.0), axis=0, keepdims=True).astype(jnp.int32)
    offset = ids - me
    offset = jnp.where(offset < 0, offset + n, offset)
    return offset, rank, rank < capacity


def exchange_kernel(
    n, groups, capacity, pad, ids_hbm, gate_hbm, tokens_hbm, cot_hbm, wup_hbm, wdn_hbm,
    back_ref, up_out, down_out, pick_out,
    ids_ref, gate_ref, tokens_ref, cot_ref, wup, wdn, send, recv, ret, hg, a_all, hg_all,
    up_acc, down_acc, pick,
    in_sem, out_sem, send_sem, recv_sem, rsend_sem, rrecv_sem,
    asend_sem, arecv_sem, hsend_sem, hrecv_sem,
):
    dp = lax.axis_index("dp")
    me = lax.axis_index("expert")
    width = tokens_ref.shape[1]
    units = wup.shape[1]
    cols = width // groups
    chunks = n // CHUNK
    lead = chunks // 2 * CHUNK
    pairs = (
        (ids_hbm, ids_ref), (tokens_hbm, tokens_ref), (gate_hbm, gate_ref), (cot_hbm, cot_ref),
        (wup_hbm, wup), (wdn_hbm, wdn),
    )
    loads = [pltpu.make_async_copy(src, dst, in_sem.at[i]) for i, (src, dst) in enumerate(pairs)]
    for copy in loads:
        copy.start()

    barrier = pltpu.get_barrier_semaphore()

    @pl.loop(1, n)
    def _(k):
        pl.semaphore_signal(
            barrier, inc=1, device_id=(dp, lax.rem(me + k, n)), device_id_type=MESH
        )

    @pl.loop(1, groups)
    def _(d):
        pl.semaphore_signal(
            barrier, inc=1, device_id=(lax.rem(dp + d, groups), me), device_id_type=MESH
        )

    loads[0].wait()
    offset, rank, kept = place(ids_ref[...], me, n, capacity)
    t = tokens_ref.shape[0]
    target = jnp.where(kept, offset * pad + rank, -1)
    select = (lax.broadcasted_iota(jnp.int32, (n * pad, t), 0) == target).astype(F32).astype(BF16)
    for copy in loads[1:4]:
        copy.wait()
    scaled = (column(gate_ref[...]) * cot_ref[...].astype(F32)).astype(BF16)
    step = 512 if width % 512 == 0 else width
    for at in range(0, width, step):
        x = jnp.dot(select, tokens_ref[:, at : at + step], preferred_element_type=F32)
        c = jnp.dot(select, scaled[:, at : at + step], preferred_element_type=F32)
        both = jnp.concatenate([x.reshape(n, pad, step), c.reshape(n, pad, step)], axis=1)
        both = both.astype(BF16)
        send[:, :, at : at + step] = both
        recv[0, :, at : at + step] = both[0]

    pl.semaphore_wait(barrier, n - 1 + groups - 1)

    def forth(k):
        return pltpu.make_async_remote_copy(
            src_ref=send.at[k], dst_ref=recv.at[k], send_sem=send_sem.at[k],
            recv_sem=recv_sem.at[k], device_id=(dp, lax.rem(me + k, n)), device_id_type=MESH,
        )

    def home(k):
        return pltpu.make_async_remote_copy(
            src_ref=ret.at[k], dst_ref=back_ref.at[k], send_sem=rsend_sem.at[k],
            recv_sem=rrecv_sem.at[k], device_id=(dp, lax.rem(me + n - k, n)), device_id_type=MESH,
        )

    def a_remote(c, d):
        peer = lax.rem(dp + d, groups)
        return pltpu.make_async_remote_copy(
            src_ref=recv.at[
                pl.ds(c * CHUNK, CHUNK), :, pl.ds(pl.multiple_of(peer * cols, 128), cols)
            ],
            dst_ref=a_all.at[d - 1, pl.ds(c * CHUNK, CHUNK)], send_sem=asend_sem.at[d - 1, c],
            recv_sem=arecv_sem.at[d - 1, c], device_id=(peer, me), device_id_type=MESH,
        )

    def h_remote(c, d):
        peer = lax.rem(dp + d, groups)
        return pltpu.make_async_remote_copy(
            src_ref=hg.at[pl.ds(c * CHUNK, CHUNK)],
            dst_ref=hg_all.at[d - 1, pl.ds(c * CHUNK, CHUNK)], send_sem=hsend_sem.at[d - 1, c],
            recv_sem=hrecv_sem.at[d - 1, c], device_id=(peer, me), device_id_type=MESH,
        )

    for k in range(lead, lead + CHUNK):
        forth(k).start()
    for k in range(1, CHUNK):
        forth(k).start()

    slots = n * 2 * pad
    there = column(jnp.where(kept, offset * (2 * pad) + rank, -2 * pad))
    slot = lax.broadcasted_iota(jnp.int32, (t, slots), 1)
    pick[0] = (slot == there).astype(F32).astype(BF16)
    pick[1] = (slot == there + pad).astype(F32).astype(BF16)
    pick_copy = pltpu.make_async_copy(pick, pick_out, out_sem.at[0])
    pick_copy.start()

    for k in range(lead, lead + CHUNK // 2):
        forth(k).wait_send()

    @pl.loop(CHUNK, n)
    def _(k):
        @pl.when((k < lead) | (k >= lead + CHUNK))
        def _():
            forth(k).start()

    for copy in loads[4:]:
        copy.wait()

    rows = CHUNK * pad
    nt = (((1,), (1,)), ((), ()))

    @pl.loop(0, chunks)
    def _(i):
        c = jnp.where(i == 0, chunks // 2, jnp.where(i <= chunks // 2, i - 1, i))

        @pl.loop(0, CHUNK)
        def _(j):
            k = c * CHUNK + j

            @pl.when(k > 0)
            def _():
                forth(k).wait_recv()

        @pl.loop(1, groups)
        def _(d):
            a_remote(c, d).start()

        a = recv[pl.ds(c * CHUNK, CHUNK)].reshape(2 * rows, width)
        pre = jnp.dot(a, wup[...], preferred_element_type=F32)
        grad = lax.dot_general(a, wdn[...], nt, preferred_element_type=F32)
        pre = pre.reshape(CHUNK, 2, pad, units)[:, 0]
        grad = grad.reshape(CHUNK, 2, pad, units)[:, 1]
        sigma = 1.0 / (1.0 + jnp.exp(-pre))
        hidden = pre * sigma
        grad = grad * sigma * (1.0 + pre * (1.0 - sigma))
        hg[pl.ds(c * CHUNK, CHUNK)] = jnp.concatenate([grad, hidden], axis=1).astype(BF16)

        @pl.loop(1, groups)
        def _(d):
            h_remote(c, d).start()

        hidden = hidden.reshape(rows, units).astype(BF16)
        grad = grad.reshape(rows, units).astype(BF16)
        for at in range(0, width, step):
            out = jnp.dot(hidden, wdn[:, at : at + step], preferred_element_type=F32)
            tok = lax.dot_general(grad, wup[at : at + step, :], nt, preferred_element_type=F32)
            both = jnp.concatenate(
                [tok.reshape(CHUNK, pad, step), out.reshape(CHUNK, pad, step)], axis=1
            )
            ret[pl.ds(c * CHUNK, CHUNK), :, at : at + step] = both.astype(BF16)

        @pl.loop(0, CHUNK)
        def _(j):
            k = c * CHUNK + j

            @pl.when(k > 0)
            def _():
                home(k).start()

    own = pltpu.make_async_copy(ret.at[0], back_ref.at[0], out_sem.at[1])
    own.start()

    inverse = 1.0 / groups
    tile = 256 if cols % 256 == 0 else cols
    tn = (((0,), (0,)), ((), ()))

    def add_group(a_tile, grads, add):
        grads = grads.reshape(slots, units)
        first = lax.rem(lax.broadcasted_iota(jnp.int32, grads.shape, 0), 2 * pad) < pad
        zero = jnp.zeros_like(grads)
        grad = jnp.where(first, grads, zero)
        hidden = jnp.where(first, zero, grads)
        for at in range(0, cols, tile):
            a = a_tile(at).reshape(slots, tile)
            up = lax.dot_general(a, grad, tn, preferred_element_type=F32) * inverse
            down = lax.dot_general(hidden, a, tn, preferred_element_type=F32) * inverse
            if add:
                up += up_acc[at : at + tile, :]
                down += down_acc[:, at : at + tile]
            up_acc[at : at + tile, :] = up
            down_acc[:, at : at + tile] = down

    add_group(
        lambda at: recv[:, :, pl.ds(pl.multiple_of(dp * cols + at, 128), tile)], hg[...], False
    )

    @pl.loop(1, groups)
    def _(d):
        @pl.loop(0, chunks)
        def _(c):
            a_remote(c, d).wait_recv()
            h_remote(c, d).wait_recv()

        add_group(lambda at: a_all[d - 1, :, :, at : at + tile], hg_all[d - 1], True)

    up_copy = pltpu.make_async_copy(up_acc, up_out, out_sem.at[2])
    down_copy = pltpu.make_async_copy(down_acc, down_out, out_sem.at[3])
    up_copy.start()
    down_copy.start()

    @pl.loop(1, groups)
    def _(d):
        @pl.loop(0, chunks)
        def _(c):
            a_remote(c, d).wait_send()
            h_remote(c, d).wait_send()

    @pl.loop(1, n)
    def _(k):
        @pl.when((k < lead) | (k >= lead + CHUNK // 2))
        def _():
            forth(k).wait_send()

        home(k).wait()

    for copy in (pick_copy, own, up_copy, down_copy):
        copy.wait()


def nbytes(arrays):
    return sum(math.prod(shape) * jnp.dtype(kind).itemsize for shape, kind in arrays)


def exchange(n, groups, capacity, pad, ids, gate, tokens, cot, wup, wdn):
    t, width = tokens.shape
    units = wup.shape[1]
    cols = width // groups
    chunks = n // CHUNK
    hbm = pl.BlockSpec(memory_space=pltpu.HBM)
    anywhere = pl.BlockSpec(memory_space=pl.ANY)
    dma = pltpu.SemaphoreType.DMA
    block = (n, 2 * pad, width)
    buffers = [
        ((1, t), jnp.int32), ((1, t), F32), ((t, width), BF16), ((t, width), BF16),
        (wup.shape, BF16), (wdn.shape, BF16), (block, BF16), (block, BF16), (block, BF16),
        ((n, 2 * pad, units), BF16),
        ((groups - 1, n, 2 * pad, cols), BF16), ((groups - 1, n, 2 * pad, units), BF16),
        ((cols, units), F32), ((units, cols), F32), ((2, t, n * 2 * pad), BF16),
    ]
    results = [
        (block, BF16), ((cols, units), F32), ((units, cols), F32), ((2, t, n * 2 * pad), BF16),
    ]
    limit = nbytes(buffers) + 10 * 2**20
    near = limit + nbytes(results) < 52 * 2**20
    place_of = pltpu.VMEM if near else jax.ShapeDtypeStruct
    return pl.pallas_call(
        functools.partial(exchange_kernel, n, groups, capacity, pad),
        out_shape=tuple(place_of(shape, kind) for shape, kind in results),
        in_specs=[hbm] * 6,
        out_specs=(anywhere,) * 4,
        scratch_shapes=[pltpu.VMEM(shape, kind) for shape, kind in buffers]
        + [
            dma((6,)), dma((4,)), dma((n,)), dma((n,)), dma((n,)), dma((n,)),
            dma((groups - 1, chunks)), dma((groups - 1, chunks)),
            dma((groups - 1, chunks)), dma((groups - 1, chunks)),
        ],
        compiler_params=pltpu.CompilerParams(
            collective_id=0, has_side_effects=True, vmem_limit_bytes=limit
        ),
        name="expert_exchange",
    )(*(pltpu.with_memory_space_constraint(x, pltpu.HBM) for x in (ids, gate, tokens, cot, wup, wdn)))


def finish_kernel(
    gate_ref, pick_ref, back_ref, up_ref, down_ref, out_ref, tok_ref, up_out, down_out,
    out_buf, tok_buf, sem, row_sem,
):
    parts = sem.shape[1]
    copies = []
    for which, (src, dst) in enumerate(((up_ref, up_out), (down_ref, down_out))):
        size = src.shape[0] // parts
        for i in range(parts):
            rows = pl.ds(i * size, size)
            copies.append(pltpu.make_async_copy(src.at[rows], dst.at[rows], sem.at[which, i]))
    for copy in copies:
        copy.start()
    gate = column(gate_ref[...])
    width = out_ref.shape[1]
    step = 512 if width % 512 == 0 else width
    for i in range(width // step):
        at = pl.ds(i * step, step)
        rows = back_ref[:, at]
        tok = jnp.dot(pick_ref[0], rows, preferred_element_type=F32).astype(BF16)
        tok_buf[:, at] = tok
        out = jnp.dot(pick_ref[1], rows, preferred_element_type=F32)
        out_buf[:, at] = (gate * out).astype(BF16)
        for j, (src, dst) in enumerate(((tok_buf, tok_ref), (out_buf, out_ref))):
            copies.append(
                pltpu.make_async_copy(src.at[:, at], dst.at[:, at], row_sem.at[j, i])
            )
            copies[-1].start()
    for copy in copies:
        copy.wait()


def finish(gate, pick, back, up, down):
    t, width = gate.shape[1], back.shape[1]
    vmem = pl.BlockSpec(memory_space=pltpu.VMEM)
    anywhere = pl.BlockSpec(memory_space=pl.ANY)
    steps = width // 512 if width % 512 == 0 else 1
    return pl.pallas_call(
        finish_kernel,
        out_shape=(
            jax.ShapeDtypeStruct((t, width), BF16),
            jax.ShapeDtypeStruct((t, width), BF16),
            jax.ShapeDtypeStruct(up.shape, F32),
            jax.ShapeDtypeStruct(down.shape, F32),
        ),
        in_specs=[vmem, vmem, vmem, anywhere, anywhere],
        out_specs=(anywhere,) * 4,
        scratch_shapes=[
            pltpu.VMEM((t, width), BF16), pltpu.VMEM((t, width), BF16),
            pltpu.SemaphoreType.DMA((2, 4)), pltpu.SemaphoreType.DMA((2, steps)),
        ],
        compiler_params=pltpu.CompilerParams(vmem_limit_bytes=16 * 2**20),
        name="finish",
    )(gate, pick, back, up, down)


def shards(tokens, expert_ids, gate, cotangent, w_up, w_down):
    t = tokens.shape[0]
    n = lax.axis_size("expert")
    groups = lax.axis_size("dp")
    capacity = t // n
    pad = -(-capacity // 8) * 8
    gate = gate[None]
    back, up, down, pick = exchange(
        n, groups, capacity, pad, expert_ids[None], gate, tokens, cotangent, w_up[0], w_down[0]
    )
    out, tok, up, down = finish(gate, pick, back.reshape(n * 2 * pad, -1), up, down)
    return out, tok, up[None], down[None]


def solution(mesh):
    in_specs = (
        P(("dp", "expert"), None),
        P(("dp", "expert")),
        P(("dp", "expert")),
        P(("dp", "expert"), None),
        P("expert", None, None),
        P("expert", None, None),
    )
    out_specs = (
        P(("dp", "expert"), None),
        P(("dp", "expert"), None),
        P("expert", "dp", None),
        P("expert", None, "dp"),
    )
    return jax.shard_map(shards, mesh=mesh, in_specs=in_specs, out_specs=out_specs, check_vma=False)
```

time: 73.7 us -> 57 us (0.77)
  the two profiles are of different devices: /device:TPU:0 before, /device:TPU:1 now
where the time goes in v2:
time: 57 us; the launch traced here: 56.8 us
  Pallas kernels  56.2 us (99%)
  between operations  0.66 us (1%)
    pallas_call x1, Pallas kernels, exchange(): pl.pallas_call(functools.partial(exchange_kernel, n, groups, capacity, pa...  53.1 us
    pallas_call x1, Pallas kernels, finish(): pl.pallas_call(finish_kernel, out_shape=(jax.ShapeDtypeStruct((t, width),...  3.1 us

profile of v2, /device:TPU:1, one launch (start us, length us, event | category | flops | bytes accessed | tf_op | source)
XLA Modules:
  0.0 56.8 jit_solution(10233403453369412402)
XLA Ops:
  0.6 0.0 copy-start
  0.6 53.1 %expert_exchange.1 = (bf16[16,16,2048]{2,1,0:T(8,128)(2,1)S(1)}, f32[1024,768]{1,0:T(8,128)S(1)}, f32[768,1024]{1,0:T(8,128)S(1)}, bf16[2,128,256]{2,1,0:T(8,128)(2,1)S(1)}) custom-call(s32[1,128]{1,0:T(1,128)} %bitcast.12, f32[1,128]{1,0:T(1,128)} %bitcast.8, bf16[128,2048]{1,0:T(8,128)(2,1)} %tokens_hbm.1, bf16[128,2048]{1,0:T(8,128)(2,1)} %cot_hbm.1, ...), custom_call_target="tpu_custom_call" | custom-call | tf_op jit(solution)/shard_map/expert_exchange/pallas_call | solution.py:284
  53.7 0.0 copy-done
  53.7 3.1 %finish.1 = (bf16[128,2048]{1,0:T(8,128)(2,1)}, bf16[128,2048]{1,0:T(8,128)(2,1)}, f32[1024,768]{1,0:T(8,128)}, f32[768,1024]{1,0:T(8,128)}) custom-call(f32[1,128]{1,0:T(1,128)S(1)} %bitcast.9, bf16[2,128,256]{2,1,0:T(8,128)(2,1)S(1)} %get-tuple-element.12.pick_ref, bf16[256,2048]{1,0:T(8,128)(2,1)S(1)} %bitcast.7, ...), custom_call_target="tpu_custom_call" | custom-call | tf_op jit(solution)/shard_map/finish/pallas_call | solution.py:339
Async XLA Ops:
  0.6 53.1 %copy-start = (f32[128]{0:T(128)S(1)}, f32[128]{0:T(128)}, u32[]{:S(2)}) copy-start(f32[128]{0:T(128)} %param.8) | copy-start | bytes 1540

commit v3 on v2

--- a/solution.py
+++ b/solution.py
@@ -36,7 +36,7 @@
 def exchange_kernel(
     n, groups, capacity, pad, ids_hbm, gate_hbm, tokens_hbm, cot_hbm, wup_hbm, wdn_hbm,
     back_ref, up_out, down_out, pick_out,
-    ids_ref, gate_ref, tokens_ref, cot_ref, wup, wdn, send, recv, ret, hg, a_all, hg_all,
+    ids_ref, gate_ref, tokens_ref, cot_ref, scaled, wup, wdn, send, recv, ret, hg, a_all, hg_all,
     up_acc, down_acc, pick,
     in_sem, out_sem, send_sem, recv_sem, rsend_sem, rrecv_sem,
     asend_sem, arecv_sem, hsend_sem, hrecv_sem,
@@ -53,7 +53,7 @@
         (wup_hbm, wup), (wdn_hbm, wdn),
     )
     loads = [pltpu.make_async_copy(src, dst, in_sem.at[i]) for i, (src, dst) in enumerate(pairs)]
-    for copy in loads:
+    for copy in loads[:4]:
         copy.start()
 
     barrier = pltpu.get_barrier_semaphore()
@@ -74,19 +74,27 @@
     offset, rank, kept = place(ids_ref[...], me, n, capacity)
     t = tokens_ref.shape[0]
     target = jnp.where(kept, offset * pad + rank, -1)
-    select = (lax.broadcasted_iota(jnp.int32, (n * pad, t), 0) == target).astype(F32).astype(BF16)
+    rows = CHUNK * pad
+    step = 512 if width % 512 == 0 else width
     for copy in loads[1:4]:
         copy.wait()
-    scaled = (column(gate_ref[...]) * cot_ref[...].astype(F32)).astype(BF16)
-    step = 512 if width % 512 == 0 else width
-    for at in range(0, width, step):
-        x = jnp.dot(select, tokens_ref[:, at : at + step], preferred_element_type=F32)
-        c = jnp.dot(select, scaled[:, at : at + step], preferred_element_type=F32)
-        both = jnp.concatenate([x.reshape(n, pad, step), c.reshape(n, pad, step)], axis=1)
-        both = both.astype(BF16)
-        send[:, :, at : at + step] = both
-        recv[0, :, at : at + step] = both[0]
-
+    for copy in loads[4:]:
+        copy.start()
+    scaled[...] = (column(gate_ref[...]) * cot_ref[...].astype(F32)).astype(BF16)
+
+    def build(c):
+        slot = lax.broadcasted_iota(jnp.int32, (rows, t), 0) + c * rows
+        select = (slot == target).astype(F32).astype(BF16)
+        for at in range(0, width, step):
+            x = jnp.dot(select, tokens_ref[:, at : at + step], preferred_element_type=F32)
+            y = jnp.dot(select, scaled[:, at : at + step], preferred_element_type=F32)
+            both = jnp.concatenate([x.reshape(CHUNK, pad, step), y.reshape(CHUNK, pad, step)], axis=1)
+            both = both.astype(BF16)
+            send[pl.ds(c * CHUNK, CHUNK), :, at : at + step] = both
+            if isinstance(c, int) and c == 0:
+                recv[0, :, at : at + step] = both[0]
+
+    build(chunks // 2)
     pl.semaphore_wait(barrier, n - 1 + groups - 1)
 
     def forth(k):
@@ -121,8 +129,15 @@
 
     for k in range(lead, lead + CHUNK):
         forth(k).start()
+    build(0)
     for k in range(1, CHUNK):
         forth(k).start()
+
+    @pl.loop(1, chunks)
+    def _(c):
+        @pl.when(c != chunks // 2)
+        def _():
+            build(c)
 
     slots = n * 2 * pad
     there = column(jnp.where(kept, offset * (2 * pad) + rank, -2 * pad))
@@ -144,7 +159,6 @@
     for copy in loads[4:]:
         copy.wait()
 
-    rows = CHUNK * pad
     nt = (((1,), (1,)), ((), ()))
 
     @pl.loop(0, chunks)
@@ -243,6 +257,9 @@
             a_remote(c, d).wait_send()
             h_remote(c, d).wait_send()
 
+    for copy in (pick_copy, own, up_copy, down_copy):
+        copy.wait()
+
     @pl.loop(1, n)
     def _(k):
         @pl.when((k < lead) | (k >= lead + CHUNK // 2))
@@ -250,9 +267,6 @@
             forth(k).wait_send()
 
         home(k).wait()
-
-    for copy in (pick_copy, own, up_copy, down_copy):
-        copy.wait()
 
 
 def nbytes(arrays):
@@ -270,7 +284,7 @@
     block = (n, 2 * pad, width)
     buffers = [
         ((1, t), jnp.int32), ((1, t), F32), ((t, width), BF16), ((t, width), BF16),
-        (wup.shape, BF16), (wdn.shape, BF16), (block, BF16), (block, BF16), (block, BF16),
+        ((t, width), BF16), (wup.shape, BF16), (wdn.shape, BF16), (block, BF16), (block, BF16), (block, BF16),
         ((n, 2 * pad, units), BF16),
         ((groups - 1, n, 2 * pad, cols), BF16), ((groups - 1, n, 2 * pad, units), BF16),
         ((cols, units), F32), ((units, cols), F32), ((2, t, n * 2 * pad), BF16),

time: 57 us -> 56.9 us (level)
  no operation moved by 1% of the time
where the time goes in v3:
time: 56.9 us; the launch traced here: 56.8 us
  Pallas kernels  56.1 us (99%)
  between operations  0.66 us (1%)
    pallas_call x1, Pallas kernels, exchange(): pl.pallas_call(functools.partial(exchange_kernel, n, groups, capacity, pa...  53 us
    pallas_call x1, Pallas kernels, finish(): pl.pallas_call(finish_kernel, out_shape=(jax.ShapeDtypeStruct((t, width),...  3.1 us

profile of v3, /device:TPU:1, one launch (start us, length us, event | category | flops | bytes accessed | tf_op | source)
XLA Modules:
  0.0 56.8 jit_solution(8325115016527699671)
XLA Ops:
  0.6 0.0 copy-start
  0.6 53.0 %expert_exchange.1 = (bf16[16,16,2048]{2,1,0:T(8,128)(2,1)S(1)}, f32[1024,768]{1,0:T(8,128)S(1)}, f32[768,1024]{1,0:T(8,128)S(1)}, bf16[2,128,256]{2,1,0:T(8,128)(2,1)S(1)}) custom-call(s32[1,128]{1,0:T(1,128)} %bitcast.12, f32[1,128]{1,0:T(1,128)} %bitcast.8, bf16[128,2048]{1,0:T(8,128)(2,1)} %tokens_hbm.1, bf16[128,2048]{1,0:T(8,128)(2,1)} %cot_hbm.1, ...), custom_call_target="tpu_custom_call" | custom-call | tf_op jit(solution)/shard_map/expert_exchange/pallas_call | solution.py:298
  53.7 0.0 copy-done
  53.7 3.1 %finish.1 = (bf16[128,2048]{1,0:T(8,128)(2,1)}, bf16[128,2048]{1,0:T(8,128)(2,1)}, f32[1024,768]{1,0:T(8,128)}, f32[768,1024]{1,0:T(8,128)}) custom-call(f32[1,128]{1,0:T(1,128)S(1)} %bitcast.9, bf16[2,128,256]{2,1,0:T(8,128)(2,1)S(1)} %get-tuple-element.12.pick_ref, bf16[256,2048]{1,0:T(8,128)(2,1)S(1)} %bitcast.7, ...), custom_call_target="tpu_custom_call" | custom-call | tf_op jit(solution)/shard_map/finish/pallas_call | solution.py:353
Async XLA Ops:
  0.6 53.1 %copy-start = (f32[128]{0:T(128)S(1)}, f32[128]{0:T(128)}, u32[]{:S(2)}) copy-start(f32[128]{0:T(128)} %param.8) | copy-start | bytes 1540

commit v4 on v3

--- a/solution.py
+++ b/solution.py
@@ -20,6 +20,14 @@
     return jnp.sum(jnp.where(eye, row, jnp.zeros_like(row)), axis=1, keepdims=True)
 
 
+def partner(me, k, n):
+    out, bit = 0, 1
+    while bit < n:
+        out = out + bit * lax.rem(me // bit + k // bit, 2)
+        bit *= 2
+    return out
+
+
 def place(ids, me, n, capacity):
     t = ids.shape[1]
     onehot = lax.broadcasted_iota(jnp.int32, (n, t), 0) == ids
@@ -28,9 +36,7 @@
         onehot.astype(F32).astype(BF16), before.astype(F32).astype(BF16), preferred_element_type=F32
     )
     rank = jnp.sum(jnp.where(onehot, counts, 0.0), axis=0, keepdims=True).astype(jnp.int32)
-    offset = ids - me
-    offset = jnp.where(offset < 0, offset + n, offset)
-    return offset, rank, rank < capacity
+    return ids ^ me, rank, rank < capacity
 
 
 def exchange_kernel(
@@ -61,7 +67,7 @@
     @pl.loop(1, n)
     def _(k):
         pl.semaphore_signal(
-            barrier, inc=1, device_id=(dp, lax.rem(me + k, n)), device_id_type=MESH
+            barrier, inc=1, device_id=(dp, partner(me, k, n)), device_id_type=MESH
         )
 
     @pl.loop(1, groups)
@@ -100,13 +106,13 @@
     def forth(k):
         return pltpu.make_async_remote_copy(
             src_ref=send.at[k], dst_ref=recv.at[k], send_sem=send_sem.at[k],
-            recv_sem=recv_sem.at[k], device_id=(dp, lax.rem(me + k, n)), device_id_type=MESH,
+            recv_sem=recv_sem.at[k], device_id=(dp, partner(me, k, n)), device_id_type=MESH,
         )
 
     def home(k):
         return pltpu.make_async_remote_copy(
             src_ref=ret.at[k], dst_ref=back_ref.at[k], send_sem=rsend_sem.at[k],
-            recv_sem=rrecv_sem.at[k], device_id=(dp, lax.rem(me + n - k, n)), device_id_type=MESH,
+            recv_sem=rrecv_sem.at[k], device_id=(dp, partner(me, k, n)), device_id_type=MESH,
         )
 
     def a_remote(c, d):
@@ -150,8 +156,10 @@
     for k in range(lead, lead + CHUNK // 2):
         forth(k).wait_send()
 
-    @pl.loop(CHUNK, n)
-    def _(k):
+    @pl.loop(0, n - CHUNK)
+    def _(i):
+        k = n - 1 - i
+
         @pl.when((k < lead) | (k >= lead + CHUNK))
         def _():
             forth(k).start()

time: 56.9 us -> 55.2 us (0.970)
  the two profiles are of different devices: /device:TPU:1 before, /device:TPU:17 now
where the time goes in v4:
time: 55.2 us; the launch traced here: 54.9 us
  Pallas kernels  54.3 us (98%)
  between operations  0.66 us (1%)
    pallas_call x1, Pallas kernels, exchange(): pl.pallas_call(functools.partial(exchange_kernel, n, groups, capacity, pa...  51.2 us
    pallas_call x1, Pallas kernels, finish(): pl.pallas_call(finish_kernel, out_shape=(jax.ShapeDtypeStruct((t, width),...  3.1 us

profile of v4, /device:TPU:17, one launch (start us, length us, event | category | flops | bytes accessed | tf_op | source)
XLA Modules:
  0.0 54.9 jit_solution(16522488880757264790)
XLA Ops:
  0.6 0.0 copy-start
  0.6 51.2 %expert_exchange.1 = (bf16[16,16,2048]{2,1,0:T(8,128)(2,1)S(1)}, f32[1024,768]{1,0:T(8,128)S(1)}, f32[768,1024]{1,0:T(8,128)S(1)}, bf16[2,128,256]{2,1,0:T(8,128)(2,1)S(1)}) custom-call(s32[1,128]{1,0:T(1,128)} %bitcast.12, f32[1,128]{1,0:T(1,128)} %bitcast.8, bf16[128,2048]{1,0:T(8,128)(2,1)} %tokens_hbm.1, bf16[128,2048]{1,0:T(8,128)(2,1)} %cot_hbm.1, ...), custom_call_target="tpu_custom_call" | custom-call | tf_op jit(solution)/shard_map/expert_exchange/pallas_call | solution.py:306
  51.8 0.0 copy-done
  51.8 3.1 %finish.1 = (bf16[128,2048]{1,0:T(8,128)(2,1)}, bf16[128,2048]{1,0:T(8,128)(2,1)}, f32[1024,768]{1,0:T(8,128)}, f32[768,1024]{1,0:T(8,128)}) custom-call(f32[1,128]{1,0:T(1,128)S(1)} %bitcast.9, bf16[2,128,256]{2,1,0:T(8,128)(2,1)S(1)} %get-tuple-element.12.pick_ref, bf16[256,2048]{1,0:T(8,128)(2,1)S(1)} %bitcast.7, ...), custom_call_target="tpu_custom_call" | custom-call | tf_op jit(solution)/shard_map/finish/pallas_call | solution.py:361
Async XLA Ops:
  0.6 51.2 %copy-start = (f32[128]{0:T(128)S(1)}, f32[128]{0:T(128)}, u32[]{:S(2)}) copy-start(f32[128]{0:T(128)} %param.8) | copy-start | bytes 1540

commit v5 on v4

--- a/solution.py
+++ b/solution.py
@@ -138,41 +138,23 @@
     build(0)
     for k in range(1, CHUNK):
         forth(k).start()
-
-    @pl.loop(1, chunks)
+    build(1)
+    for k in range(CHUNK, 2 * CHUNK):
+        forth(k).start()
+
+    @pl.loop(2, chunks)
     def _(c):
         @pl.when(c != chunks // 2)
         def _():
             build(c)
 
-    slots = n * 2 * pad
-    there = column(jnp.where(kept, offset * (2 * pad) + rank, -2 * pad))
-    slot = lax.broadcasted_iota(jnp.int32, (t, slots), 1)
-    pick[0] = (slot == there).astype(F32).astype(BF16)
-    pick[1] = (slot == there + pad).astype(F32).astype(BF16)
-    pick_copy = pltpu.make_async_copy(pick, pick_out, out_sem.at[0])
-    pick_copy.start()
-
-    for k in range(lead, lead + CHUNK // 2):
-        forth(k).wait_send()
-
-    @pl.loop(0, n - CHUNK)
-    def _(i):
-        k = n - 1 - i
-
-        @pl.when((k < lead) | (k >= lead + CHUNK))
-        def _():
-            forth(k).start()
-
     for copy in loads[4:]:
         copy.wait()
 
     nt = (((1,), (1,)), ((), ()))
 
     @pl.loop(0, chunks)
-    def _(i):
-        c = jnp.where(i == 0, chunks // 2, jnp.where(i <= chunks // 2, i - 1, i))
-
+    def _(c):
         @pl.loop(0, CHUNK)
         def _(j):
             k = c * CHUNK + j
@@ -216,6 +198,23 @@
             @pl.when(k > 0)
             def _():
                 home(k).start()
+
+        @pl.when(c < 2)
+        def _():
+            @pl.loop(2, chunks)
+            def _(later):
+                @pl.when(later != chunks // 2)
+                def _():
+                    for j in range(CHUNK // 2):
+                        forth(later * CHUNK + c * (CHUNK // 2) + j).start()
+
+    slots = n * 2 * pad
+    there = column(jnp.where(kept, offset * (2 * pad) + rank, -2 * pad))
+    slot = lax.broadcasted_iota(jnp.int32, (t, slots), 1)
+    pick[0] = (slot == there).astype(F32).astype(BF16)
+    pick[1] = (slot == there + pad).astype(F32).astype(BF16)
+    pick_copy = pltpu.make_async_copy(pick, pick_out, out_sem.at[0])
+    pick_copy.start()
 
     own = pltpu.make_async_copy(ret.at[0], back_ref.at[0], out_sem.at[1])
     own.start()
@@ -270,10 +269,7 @@
 
     @pl.loop(1, n)
     def _(k):
-        @pl.when((k < lead) | (k >= lead + CHUNK // 2))
-        def _():
-            forth(k).wait_send()
-
+        forth(k).wait_send()
         home(k).wait()
 
 

time: 55.2 us -> 57.8 us (1.047)
  Pallas kernels: 54.3 us -> 57 us
    pallas_call x1, Pallas kernels: 51.2 us -> 53.9 us  [exchange(): pl.pallas_call(functools.partial(exchange_kernel, n, groups, capacity, pa...]
where the time goes in v5:
time: 57.8 us; the launch traced here: 57.7 us
  Pallas kernels  57 us (99%)
  between operations  0.66 us (1%)
    pallas_call x1, Pallas kernels, exchange(): pl.pallas_call(functools.partial(exchange_kernel, n, groups, capacity, pa...  53.9 us
    pallas_call x1, Pallas kernels, finish(): pl.pallas_call(finish_kernel, out_shape=(jax.ShapeDtypeStruct((t, width),...  3.1 us

profile of v5, /device:TPU:17, one launch (start us, length us, event | category | flops | bytes accessed | tf_op | source)
XLA Modules:
  0.0 57.7 jit_solution(207029698712826683)
XLA Ops:
  0.6 0.0 copy-start
  0.6 53.9 %expert_exchange.1 = (bf16[16,16,2048]{2,1,0:T(8,128)(2,1)S(1)}, f32[1024,768]{1,0:T(8,128)S(1)}, f32[768,1024]{1,0:T(8,128)S(1)}, bf16[2,128,256]{2,1,0:T(8,128)(2,1)S(1)}) custom-call(s32[1,128]{1,0:T(1,128)} %bitcast.12, f32[1,128]{1,0:T(1,128)} %bitcast.8, bf16[128,2048]{1,0:T(8,128)(2,1)} %tokens_hbm.1, bf16[128,2048]{1,0:T(8,128)(2,1)} %cot_hbm.1, ...), custom_call_target="tpu_custom_call" | custom-call | tf_op jit(solution)/shard_map/expert_exchange/pallas_call | solution.py:302
  54.6 0.0 copy-done
  54.6 3.1 %finish.1 = (bf16[128,2048]{1,0:T(8,128)(2,1)}, bf16[128,2048]{1,0:T(8,128)(2,1)}, f32[1024,768]{1,0:T(8,128)}, f32[768,1024]{1,0:T(8,128)}) custom-call(f32[1,128]{1,0:T(1,128)S(1)} %bitcast.9, bf16[2,128,256]{2,1,0:T(8,128)(2,1)S(1)} %get-tuple-element.12.pick_ref, bf16[256,2048]{1,0:T(8,128)(2,1)S(1)} %bitcast.7, ...), custom_call_target="tpu_custom_call" | custom-call | tf_op jit(solution)/shard_map/finish/pallas_call | solution.py:357
Async XLA Ops:
  0.6 53.9 %copy-start = (f32[128]{0:T(128)S(1)}, f32[128]{0:T(128)}, u32[]{:S(2)}) copy-start(f32[128]{0:T(128)} %param.8) | copy-start | bytes 1540

commit v6 on v4

--- a/solution.py
+++ b/solution.py
@@ -53,7 +53,10 @@
     units = wup.shape[1]
     cols = width // groups
     chunks = n // CHUNK
-    lead = chunks // 2 * CHUNK
+    quarter = me // (n // 4)
+    middle = (quarter == 1) | (quarter == 2)
+    first = jnp.where(middle, chunks - chunks // 4, chunks // 2)
+    lead = first * CHUNK
     pairs = (
         (ids_hbm, ids_ref), (tokens_hbm, tokens_ref), (gate_hbm, gate_ref), (cot_hbm, cot_ref),
         (wup_hbm, wup), (wdn_hbm, wdn),
@@ -100,7 +103,7 @@
             if isinstance(c, int) and c == 0:
                 recv[0, :, at : at + step] = both[0]
 
-    build(chunks // 2)
+    build(first)
     pl.semaphore_wait(barrier, n - 1 + groups - 1)
 
     def forth(k):
@@ -133,15 +136,18 @@
             recv_sem=hrecv_sem.at[d - 1, c], device_id=(peer, me), device_id_type=MESH,
         )
 
-    for k in range(lead, lead + CHUNK):
-        forth(k).start()
+    for j in range(CHUNK):
+        forth(lead + j).start()
     build(0)
     for k in range(1, CHUNK):
         forth(k).start()
-
-    @pl.loop(1, chunks)
+    build(1)
+    for k in range(CHUNK, 2 * CHUNK):
+        forth(k).start()
+
+    @pl.loop(2, chunks)
     def _(c):
-        @pl.when(c != chunks // 2)
+        @pl.when(c != first)
         def _():
             build(c)
 
@@ -153,10 +159,10 @@
     pick_copy = pltpu.make_async_copy(pick, pick_out, out_sem.at[0])
     pick_copy.start()
 
-    for k in range(lead, lead + CHUNK // 2):
-        forth(k).wait_send()
-
-    @pl.loop(0, n - CHUNK)
+    for j in range(CHUNK // 2):
+        forth(lead + j).wait_send()
+
+    @pl.loop(0, n - 2 * CHUNK)
     def _(i):
         k = n - 1 - i
 
@@ -171,7 +177,9 @@
 
     @pl.loop(0, chunks)
     def _(i):
-        c = jnp.where(i == 0, chunks // 2, jnp.where(i <= chunks // 2, i - 1, i))
+        half = chunks // 2
+        ends = jnp.where(i < half, i, chunks - 1 - (i - half))
+        c = jnp.where(middle, lax.rem(i + half, chunks), ends)
 
         @pl.loop(0, CHUNK)
         def _(j):

time: 55.2 us -> 56.4 us (1.022)
  Pallas kernels: 54.3 us -> 55 us
    pallas_call x1, Pallas kernels: 51.2 us -> 51.9 us  [exchange(): pl.pallas_call(functools.partial(exchange_kernel, n, groups, capacity, pa...]
where the time goes in v6:
time: 56.4 us; the launch traced here: 55.6 us
  Pallas kernels  55 us (98%)
  between operations  0.66 us (1%)
    pallas_call x1, Pallas kernels, exchange(): pl.pallas_call(functools.partial(exchange_kernel, n, groups, capacity, pa...  51.9 us
    pallas_call x1, Pallas kernels, finish(): pl.pallas_call(finish_kernel, out_shape=(jax.ShapeDtypeStruct((t, width),...  3.1 us

profile of v6, /device:TPU:17, one launch (start us, length us, event | category | flops | bytes accessed | tf_op | source)
XLA Modules:
  0.0 55.6 jit_solution(3837833282728006117)
XLA Ops:
  0.6 0.0 copy-start
  0.6 51.9 %expert_exchange.1 = (bf16[16,16,2048]{2,1,0:T(8,128)(2,1)S(1)}, f32[1024,768]{1,0:T(8,128)S(1)}, f32[768,1024]{1,0:T(8,128)S(1)}, bf16[2,128,256]{2,1,0:T(8,128)(2,1)S(1)}) custom-call(s32[1,128]{1,0:T(1,128)} %bitcast.12, f32[1,128]{1,0:T(1,128)} %bitcast.8, bf16[128,2048]{1,0:T(8,128)(2,1)} %tokens_hbm.1, bf16[128,2048]{1,0:T(8,128)(2,1)} %cot_hbm.1, ...), custom_call_target="tpu_custom_call" | custom-call | tf_op jit(solution)/shard_map/expert_exchange/pallas_call | solution.py:314
  52.5 0.0 copy-done
  52.5 3.1 %finish.1 = (bf16[128,2048]{1,0:T(8,128)(2,1)}, bf16[128,2048]{1,0:T(8,128)(2,1)}, f32[1024,768]{1,0:T(8,128)}, f32[768,1024]{1,0:T(8,128)}) custom-call(f32[1,128]{1,0:T(1,128)S(1)} %bitcast.9, bf16[2,128,256]{2,1,0:T(8,128)(2,1)S(1)} %get-tuple-element.12.pick_ref, bf16[256,2048]{1,0:T(8,128)(2,1)S(1)} %bitcast.7, ...), custom_call_target="tpu_custom_call" | custom-call | tf_op jit(solution)/shard_map/finish/pallas_call | solution.py:369
Async XLA Ops:
  0.6 51.9 %copy-start = (f32[128]{0:T(128)S(1)}, f32[128]{0:T(128)}, u32[]{:S(2)}) copy-start(f32[128]{0:T(128)} %param.8) | copy-start | bytes 1540

commit v7 on v4

--- a/solution.py
+++ b/solution.py
@@ -145,6 +145,81 @@
         def _():
             build(c)
 
+    for k in range(lead, lead + CHUNK // 2):
+        forth(k).wait_send()
+
+    @pl.loop(0, n - CHUNK)
+    def _(i):
+        k = n - 1 - i
+
+        @pl.when((k < lead) | (k >= lead + CHUNK))
+        def _():
+            forth(k).start()
+
+    for copy in loads[4:]:
+        copy.wait()
+
+    nt = (((1,), (1,)), ((), ()))
+
+    def serve(c, m):
+        count = m * CHUNK
+        held = pl.ds(c * CHUNK, count)
+
+        @pl.loop(0, count)
+        def _(j):
+            k = c * CHUNK + j
+
+            @pl.when(k > 0)
+            def _():
+                forth(k).wait_recv()
+
+        @pl.loop(1, groups)
+        def _(d):
+            for i in range(m):
+                a_remote(c + i, d).start()
+
+        a = recv[held].reshape(m * 2 * rows, width)
+        pre = jnp.dot(a, wup[...], preferred_element_type=F32)
+        grad = lax.dot_general(a, wdn[...], nt, preferred_element_type=F32)
+        pre = pre.reshape(count, 2, pad, units)[:, 0]
+        grad = grad.reshape(count, 2, pad, units)[:, 1]
+        sigma = 1.0 / (1.0 + jnp.exp(-pre))
+        hidden = pre * sigma
+        grad = grad * sigma * (1.0 + pre * (1.0 - sigma))
+        hg[held] = jnp.concatenate([grad, hidden], axis=1).astype(BF16)
+
+        @pl.loop(1, groups)
+        def _(d):
+            for i in range(m):
+                h_remote(c + i, d).start()
+
+        hidden = hidden.reshape(m * rows, units).astype(BF16)
+        grad = grad.reshape(m * rows, units).astype(BF16)
+        for at in range(0, width, step):
+            out = jnp.dot(hidden, wdn[:, at : at + step], preferred_element_type=F32)
+            tok = lax.dot_general(grad, wup[at : at + step, :], nt, preferred_element_type=F32)
+            both = jnp.concatenate(
+                [tok.reshape(count, pad, step), out.reshape(count, pad, step)], axis=1
+            )
+            ret[held, :, at : at + step] = both.astype(BF16)
+
+        @pl.loop(0, count)
+        def _(j):
+            k = c * CHUNK + j
+
+            @pl.when(k > 0)
+            def _():
+                home(k).start()
+
+    serve(chunks // 2, 1)
+    serve(0, 2)
+
+    @pl.loop(2, chunks)
+    def _(c):
+        @pl.when(c != chunks // 2)
+        def _():
+            serve(c, 1)
+
     slots = n * 2 * pad
     there = column(jnp.where(kept, offset * (2 * pad) + rank, -2 * pad))
     slot = lax.broadcasted_iota(jnp.int32, (t, slots), 1)
@@ -152,70 +227,6 @@
     pick[1] = (slot == there + pad).astype(F32).astype(BF16)
     pick_copy = pltpu.make_async_copy(pick, pick_out, out_sem.at[0])
     pick_copy.start()
-
-    for k in range(lead, lead + CHUNK // 2):
-        forth(k).wait_send()
-
-    @pl.loop(0, n - CHUNK)
-    def _(i):
-        k = n - 1 - i
-
-        @pl.when((k < lead) | (k >= lead + CHUNK))
-        def _():
-            forth(k).start()
-
-    for copy in loads[4:]:
-        copy.wait()
-
-    nt = (((1,), (1,)), ((), ()))
-
-    @pl.loop(0, chunks)
-    def _(i):
-        c = jnp.where(i == 0, chunks // 2, jnp.where(i <= chunks // 2, i - 1, i))
-
-        @pl.loop(0, CHUNK)
-        def _(j):
-            k = c * CHUNK + j
-
-            @pl.when(k > 0)
-            def _():
-                forth(k).wait_recv()
-
-        @pl.loop(1, groups)
-        def _(d):
-            a_remote(c, d).start()
-
-        a = recv[pl.ds(c * CHUNK, CHUNK)].reshape(2 * rows, width)
-        pre = jnp.dot(a, wup[...], preferred_element_type=F32)
-        grad = lax.dot_general(a, wdn[...], nt, preferred_element_type=F32)
-        pre = pre.reshape(CHUNK, 2, pad, units)[:, 0]
-        grad = grad.reshape(CHUNK, 2, pad, units)[:, 1]
-        sigma = 1.0 / (1.0 + jnp.exp(-pre))
-        hidden = pre * sigma
-        grad = grad * sigma * (1.0 + pre * (1.0 - sigma))
-        hg[pl.ds(c * CHUNK, CHUNK)] = jnp.concatenate([grad, hidden], axis=1).astype(BF16)
-
-        @pl.loop(1, groups)
-        def _(d):
-            h_remote(c, d).start()
-
-        hidden = hidden.reshape(rows, units).astype(BF16)
-        grad = grad.reshape(rows, units).astype(BF16)
-        for at in range(0, width, step):
-            out = jnp.dot(hidden, wdn[:, at : at + step], preferred_element_type=F32)
-            tok = lax.dot_general(grad, wup[at : at + step, :], nt, preferred_element_type=F32)
-            both = jnp.concatenate(
-                [tok.reshape(CHUNK, pad, step), out.reshape(CHUNK, pad, step)], axis=1
-            )
-            ret[pl.ds(c * CHUNK, CHUNK), :, at : at + step] = both.astype(BF16)
-
-        @pl.loop(0, CHUNK)
-        def _(j):
-            k = c * CHUNK + j
-
-            @pl.when(k > 0)
-            def _():
-                home(k).start()
 
     own = pltpu.make_async_copy(ret.at[0], back_ref.at[0], out_sem.at[1])
     own.start()

time: 55.2 us -> 55.1 us (level)
  no operation moved by 1% of the time
where the time goes in v7:
time: 55.1 us; the launch traced here: 54.9 us
  Pallas kernels  54.3 us (99%)
  between operations  0.66 us (1%)
    pallas_call x1, Pallas kernels, exchange(): pl.pallas_call(functools.partial(exchange_kernel, n, groups, capacity, pa...  51.2 us
    pallas_call x1, Pallas kernels, finish(): pl.pallas_call(finish_kernel, out_shape=(jax.ShapeDtypeStruct((t, width),...  3.1 us

profile of v7, /device:TPU:17, one launch (start us, length us, event | category | flops | bytes accessed | tf_op | source)
XLA Modules:
  0.0 54.9 jit_solution(15841302618977784688)
XLA Ops:
  0.6 0.0 copy-start
  0.6 51.2 %expert_exchange.1 = (bf16[16,16,2048]{2,1,0:T(8,128)(2,1)S(1)}, f32[1024,768]{1,0:T(8,128)S(1)}, f32[768,1024]{1,0:T(8,128)S(1)}, bf16[2,128,256]{2,1,0:T(8,128)(2,1)S(1)}) custom-call(s32[1,128]{1,0:T(1,128)} %bitcast.12, f32[1,128]{1,0:T(1,128)} %bitcast.8, bf16[128,2048]{1,0:T(8,128)(2,1)} %tokens_hbm.1, bf16[128,2048]{1,0:T(8,128)(2,1)} %cot_hbm.1, ...), custom_call_target="tpu_custom_call" | custom-call | tf_op jit(solution)/shard_map/expert_exchange/pallas_call | solution.py:317
  51.8 0.0 copy-done
  51.8 3.1 %finish.1 = (bf16[128,2048]{1,0:T(8,128)(2,1)}, bf16[128,2048]{1,0:T(8,128)(2,1)}, f32[1024,768]{1,0:T(8,128)}, f32[768,1024]{1,0:T(8,128)}) custom-call(f32[1,128]{1,0:T(1,128)S(1)} %bitcast.9, bf16[2,128,256]{2,1,0:T(8,128)(2,1)S(1)} %get-tuple-element.12.pick_ref, bf16[256,2048]{1,0:T(8,128)(2,1)S(1)} %bitcast.7, ...), custom_call_target="tpu_custom_call" | custom-call | tf_op jit(solution)/shard_map/finish/pallas_call | solution.py:372
Async XLA Ops:
  0.6 51.2 %copy-start = (f32[128]{0:T(128)S(1)}, f32[128]{0:T(128)}, u32[]{:S(2)}) copy-start(f32[128]{0:T(128)} %param.8) | copy-start | bytes 1540

commit v8 on v7

--- a/solution.py
+++ b/solution.py
@@ -54,6 +54,8 @@
     cols = width // groups
     chunks = n // CHUNK
     lead = chunks // 2 * CHUNK
+    quarter = me // (n // 4)
+    middle = (quarter == 1) | (quarter == 2)
     pairs = (
         (ids_hbm, ids_ref), (tokens_hbm, tokens_ref), (gate_hbm, gate_ref), (cot_hbm, cot_ref),
         (wup_hbm, wup), (wdn_hbm, wdn),
@@ -145,8 +147,10 @@
         def _():
             build(c)
 
-    for k in range(lead, lead + CHUNK // 2):
-        forth(k).wait_send()
+    @pl.when(jnp.logical_not(middle))
+    def _():
+        for k in range(lead, lead + CHUNK // 2):
+            forth(k).wait_send()
 
     @pl.loop(0, n - CHUNK)
     def _(i):
@@ -281,7 +285,7 @@
 
     @pl.loop(1, n)
     def _(k):
-        @pl.when((k < lead) | (k >= lead + CHUNK // 2))
+        @pl.when(middle | (k < lead) | (k >= lead + CHUNK // 2))
         def _():
             forth(k).wait_send()
 

time: 55.1 us -> 55.1 us (level)
  no operation moved by 1% of the time
where the time goes in v8:
time: 55.1 us; the launch traced here: 54.9 us
  Pallas kernels  54.2 us (98%)
  between operations  0.66 us (1%)
    pallas_call x1, Pallas kernels, exchange(): pl.pallas_call(functools.partial(exchange_kernel, n, groups, capacity, pa...  51.1 us
    pallas_call x1, Pallas kernels, finish(): pl.pallas_call(finish_kernel, out_shape=(jax.ShapeDtypeStruct((t, width),...  3.1 us

profile of v8, /device:TPU:17, one launch (start us, length us, event | category | flops | bytes accessed | tf_op | source)
XLA Modules:
  0.0 54.9 jit_solution(1442228451495706105)
XLA Ops:
  0.6 0.0 copy-start
  0.6 51.1 %expert_exchange.1 = (bf16[16,16,2048]{2,1,0:T(8,128)(2,1)S(1)}, f32[1024,768]{1,0:T(8,128)S(1)}, f32[768,1024]{1,0:T(8,128)S(1)}, bf16[2,128,256]{2,1,0:T(8,128)(2,1)S(1)}) custom-call(s32[1,128]{1,0:T(1,128)} %bitcast.12, f32[1,128]{1,0:T(1,128)} %bitcast.8, bf16[128,2048]{1,0:T(8,128)(2,1)} %tokens_hbm.1, bf16[128,2048]{1,0:T(8,128)(2,1)} %cot_hbm.1, ...), custom_call_target="tpu_custom_call" | custom-call | tf_op jit(solution)/shard_map/expert_exchange/pallas_call | solution.py:321
  51.7 0.0 copy-done
  51.8 3.1 %finish.1 = (bf16[128,2048]{1,0:T(8,128)(2,1)}, bf16[128,2048]{1,0:T(8,128)(2,1)}, f32[1024,768]{1,0:T(8,128)}, f32[768,1024]{1,0:T(8,128)}) custom-call(f32[1,128]{1,0:T(1,128)S(1)} %bitcast.9, bf16[2,128,256]{2,1,0:T(8,128)(2,1)S(1)} %get-tuple-element.12.pick_ref, bf16[256,2048]{1,0:T(8,128)(2,1)S(1)} %bitcast.7, ...), custom_call_target="tpu_custom_call" | custom-call | tf_op jit(solution)/shard_map/finish/pallas_call | solution.py:376
Async XLA Ops:
  0.6 51.1 %copy-start = (f32[128]{0:T(128)S(1)}, f32[128]{0:T(128)}, u32[]{:S(2)}) copy-start(f32[128]{0:T(128)} %param.8) | copy-start | bytes 1540
